TPU v7x, 256 devices: a whole 4x4x8 slice. The times are simulated.
256 devices in a mesh: ctx: 16 (over z_lo, y, core), tp: 16 (over x, z_hi).
Axes of the slice: x: 4, y: 4, z: 8 (z_hi: 4, z_lo: 2; z = z_hi * 2 + z_lo), core: 2. Of those that a mesh axis runs over, the one named last changes fastest.
Arguments:
- tokens: bfloat16 [4096, 4096], P('ctx', 'tp'), may hold values from -6 to 6
- cotangent: bfloat16 [4096, 4096], P('ctx', 'tp'), may hold values from -6 to 6
- norm_gain: bfloat16 [4096], P('tp'), may hold values from 0.25 to 1.75
- in_weight: bfloat16 [4096, 3, 4096], P(None, None, 'tp'), may hold values from -0.09375 to 0.09375
- in_down: bfloat16 [4096, 256], P('tp'), may hold values from -0.09375 to 0.09375
- in_up: bfloat16 [256, 3, 4096], P(None, None, 'tp'), may hold values from -0.375 to 0.375
- in_scale: float32 [3, 4096], P(None, 'tp'), may hold values from -3 to 3
- scale_table: float32 [4, 256], replicated, may hold values from -4 to 4
- table_pick: int32 [4], replicated, may hold values from 0 to 3
- short_taps: float32 [3, 3, 4096], P(None, None, 'tp'), may hold values from -3.5 to 3.5
- residue: float32 [4096], P('tp'), may hold values from -3 to 3
- decay: float32 [4096], P('tp'), may hold values from 1.2207031e-05 to 0.0333333333
- skip_gain: float32 [4096], P('tp'), may hold values from 0.5 to 1.5
- out_weight: bfloat16 [4096, 4096], P('tp'), may hold values from -0.09375 to 0.09375
- out_down: bfloat16 [4096, 256], P('tp'), may hold values from -0.09375 to 0.09375
- out_up: bfloat16 [256, 4096], P(None, 'tp'), may hold values from -0.375 to 0.375
- out_scale: float32 [4096], P('tp'), may hold values from -3 to 3
Outputs:
- mixed: bfloat16 [4096, 4096], P('ctx', 'tp')
- grad_tokens: bfloat16 [4096, 4096], P('ctx', 'tp')
- grad_table: float32 [4, 256], replicated
- grad_in_scale: float32 [3, 4096], P(None, 'tp')
- grad_out_scale: float32 [4096], P('tp')
All inputs are finite; a program needn't handle non-finite values.
Results may differ from a plain program's by a relative error of at most 0.039.
Values may be sent and summed in bfloat16 or wider, within the bound.
No kernel may reach another device: no remote copies, remote signals or barrier semaphores. Data moves between devices by JAX's collectives and lax.ppermute only.
A program may use at most 64 MiB of HBM per device.

v0:
```python
import jax
import jax.numpy as jnp
from jax import lax
from jax.experimental import pallas as pl
from jax.experimental.pallas import tpu as pltpu
from jax.sharding import Mesh, PartitionSpec as P

HIGH = lax.Precision.HIGHEST
CTX = ("zl", "y", "core")
TP = ("x", "zh")
F32 = jnp.float32
BF16 = jnp.bfloat16
T = 256
C = 256
RANK = 256
SLABS = 16
LOW_T = 272
CUT_T = 144
CUT = 128
WIDTH = 4096
KAP, DEC, SKIP, SCALE, TAPS, PICKED = 0, 1, 2, 3, 6, 15


def shift(v, axis, k):
    return lax.ppermute(v, axis, [(i, (i + k) % 4) for i in range(4)])


def swap(v, axis):
    return lax.ppermute(v, axis, [(0, 1), (1, 0)])


def stack(*parts):
    def kernel(*refs):
        for i, ref in enumerate(refs[:-1]):
            refs[-1][i] = ref[...]

    return call(kernel, [((len(parts),) + parts[0].shape, parts[0].dtype)], parts)[0]


def ctx_gather(v):
    first = stack(v, swap(v, "core"))
    v = stack(first, across(first, "y", 1))
    v = stack(v, across(v, "y", 2))
    return [v, swap(v, "zl")], first


def across(v, axis, bit):
    return lax.ppermute(v, axis, [(i, i ^ bit) for i in range(4)])


def ctx_spread(v):
    wide = jnp.broadcast_to(v[None], (SLABS,) + v.shape)
    return lax.all_to_all(wide, CTX, split_axis=0, concat_axis=0, tiled=True)


def place(scr, near, other):
    zl, y, core = (lax.axis_index(a) for a in CTX)
    for kz, src in enumerate((near, other)):
        for ky in range(4):
            for kc in range(2):
                slab = (1 - zl if kz else zl) * 8 + jnp.bitwise_xor(y, ky) * 2
                slab = slab + (1 - core if kc else core)
                scr[slab] = src[ky // 2, ky % 2, kc]


def position():
    zl, y, core = (lax.axis_index(a) for a in CTX)
    return zl * 8 + y * 2 + core


def block_ids():
    x, zh = lax.axis_index("x"), lax.axis_index("zh")
    xs = [x, lax.rem(x + 3, 4), lax.rem(x + 1, 4), lax.rem(x + 2, 4)]
    zs = [jnp.bitwise_xor(zh, r) for r in range(4)]
    return [[a * 4 + b for b in zs] for a in xs]


def x_gather(own):
    return [own, shift(own, "x", 1), shift(own, "x", -1), shift(own, "x", 2)]


def ring_gather(own, cut):
    left, right = shift(own, "x", 1), shift(own, "x", -1)
    rows = own.shape[0]

    def kernel(left_ref, right_ref, fa, fb):
        fa[...] = left_ref[0:cut, :]
        fb[...] = right_ref[cut:rows, :]

    shapes = [((cut, C), BF16), ((rows - cut, C), BF16)]
    fa, fb = call(kernel, shapes, [left, right])
    return [own, left, right, shift(fa, "x", 1), shift(fb, "x", -1)]


def x_scatter(right, left, far):
    return [shift(right, "x", 1), shift(left, "x", -1), shift(far, "x", 2)]


def as_pairs(quad, cut):
    return [(g.at[0:cut, :], g.at[cut:, :]) for g in quad]


def dot(a, b):
    return jnp.dot(a, b, preferred_element_type=F32)


def dot_nt(a, b):
    return lax.dot_general(a, b, (((1,), (1,)), ((), ())), preferred_element_type=F32)


def rnd(v):
    return v.astype(BF16).astype(F32)


def row_ids():
    return lax.broadcasted_iota(jnp.int32, (T, C), 0)


def column(row):
    square = (T, T)
    same = lax.broadcasted_iota(jnp.int32, square, 0) == lax.broadcasted_iota(jnp.int32, square, 1)
    return jnp.sum(jnp.where(same, row, 0.0), axis=1, keepdims=True)


def line(col):
    square = (T, T)
    same = lax.broadcasted_iota(jnp.int32, square, 0) == lax.broadcasted_iota(jnp.int32, square, 1)
    return jnp.sum(jnp.where(same, col, 0.0), axis=0, keepdims=True)


def thirds(row):
    hi = rnd(row)
    mid = rnd(row - hi)
    return [hi, mid, row - hi - mid]


def tile_of(rows, n=16):
    at = lax.broadcasted_iota(jnp.int32, (n, C), 0)
    out = jnp.zeros((n, C), F32)
    for i, row in enumerate(rows):
        out = jnp.where(at == i, row, out)
    return out.astype(BF16)


def joined(tile, i):
    return tile[i : i + 1] + tile[i + 1 : i + 2] + tile[i + 2 : i + 3]


def down(v, n, rows):
    return jnp.where(rows >= n, pltpu.roll(v, n, 0), 0.0)


def up(v, n, rows):
    return jnp.where(rows < T - n, pltpu.roll(v, T - n, 0), 0.0)


def scan_down(v, dec, rows):
    for k in range(8):
        n = 1 << k
        v = v + jnp.exp(-dec * n) * down(v, n, rows)
    return v


def scan_up(v, dec, rows):
    for k in range(8):
        n = 1 << k
        v = v + jnp.exp(-dec * n) * up(v, n, rows)
    return v


def row_of(ref, n):
    return ref[n : n + 1, :]


def blk(a_ref, b_ref, r, head):
    if r < 2:
        return a_ref[r * 256 : r * 256 + 256, :]
    at = head + (r - 2) * 256
    return b_ref[at : at + 256, :]


def put_blk(a_ref, b_ref, r, head, v):
    if r < 2:
        a_ref[r * 256 : r * 256 + 256, :] = v
    else:
        at = head + (r - 2) * 256
        b_ref[at : at + 256, :] = v


def low_sum(pairs, cut, low):
    out = []
    for part, size in ((0, cut), (1, low - cut)):
        at = 512 if part == 0 else 0
        v = 0.0
        for pair in pairs:
            v = v + pair[part][at : at + size, :].astype(F32)
        out.append(v)
    return jnp.concatenate(out, 0)


def const_kernel(pick, kap, dec, skip, scale, taps, table, cst):
    cst[0:1, :] = kap[...]
    cst[1:2, :] = dec[...]
    cst[2:3, :] = skip[...]
    cst[3:6, :] = scale[...]
    for i in range(3):
        for j in range(3):
            cst[TAPS + 3 * i + j : TAPS + 3 * i + j + 1, :] = taps[i, j : j + 1, :]
    for i in range(4):
        row = jnp.zeros((1, RANK), F32)
        for g in range(4):
            chosen = jnp.full((1, RANK), pick[i], jnp.int32) == g
            row = row + jnp.where(chosen, table[g : g + 1, :], 0.0)
        cst[PICKED + i : PICKED + i + 1, :] = row
    cst[19:24, :] = jnp.zeros((5, C), F32)


def cot_start_kernel(cot, upw, scale, after, pay):
    pay[0:256, :] = cot[...]
    pay[256:512, :] = upw[...]
    at = lax.broadcasted_iota(jnp.int32, (16, C), 0)
    rows = after[512:528, :].astype(F32)
    for i, row in enumerate(thirds(scale[...])):
        rows = jnp.where(at == i, row, rows)
    pay[512:528, :] = rows.astype(BF16)


def token_kernel(z0, z1, z2, z3, out):
    a_ref, b_ref = out.at[0:656, :], out.at[656:1296, :]
    low = jnp.zeros((T, RANK), F32)
    squares = jnp.zeros((T, 1), F32)
    for r, z in enumerate((z0, z1, z2, z3)):
        x = z[:256, :].astype(F32)
        gain = z[512:528, :].astype(F32)[:1]
        xg = (x * gain).astype(BF16)
        put_blk(a_ref, b_ref, r, 128, xg)
        low = low + dot(xg, z[256:512, :])
        squares = squares + jnp.sum(x * x, axis=1, keepdims=True)
    low = low.astype(BF16)
    a_ref[512:656, :] = low[:144]
    b_ref[0:112, :] = low[144:]
    b_ref[112:128, :] = tile_of(thirds(line(squares)))


def cot_kernel(z0, z1, z2, z3, out):
    a_ref, b_ref = out.at[0:640, :], out.at[640:1280, :]
    low = jnp.zeros((T, RANK), F32)
    for r, z in enumerate((z0, z1, z2, z3)):
        cot = z[:256, :]
        scale = joined(z[512:528, :].astype(F32), 0)
        put_blk(a_ref, b_ref, r, 128, cot)
        low = low + dot_nt((cot.astype(F32) * scale).astype(BF16), z[256:512, :])
    low = low.astype(BF16)
    a_ref[512:640, :] = low[:128]
    b_ref[0:128, :] = low[128:]


def fwd_in_kernel(
    g0, g1, g2, ga, gb, w_ref, up_ref, cst,
    zraw_ref, z_ref, zlow_ref, h_ref, edge_ref, low_ref, rstd_ref,
):
    rows = row_ids()
    ids = block_ids()
    pairs = as_pairs((g0, g1, g2), 656) + [(ga, gb)]
    total = low_sum(pairs, CUT_T, LOW_T)
    rstd = column(lax.rsqrt(joined(total[256:], 0) / WIDTH + 1e-06))
    rstd_ref[...] = rstd
    low_ref[...] = total[:256]
    low_in = low_ref[...] * rstd
    dec = row_of(cst, DEC)
    feat = []
    for i in range(3):
        acc = jnp.zeros((T, C), F32)
        for k, pair in enumerate(pairs):
            for r in range(4):
                acc = acc + dot(blk(*pair, r, 128), w_ref[i, ids[k][r]])
        zraw_ref[i] = acc
        zlow = dot((low_in * row_of(cst, PICKED + i)).astype(BF16), up_ref[i])
        zlow_ref[i] = zlow
        z = (acc * rstd + zlow * row_of(cst, SCALE + i)).astype(BF16)
        z_ref[i] = z
        z = z.astype(F32)
        edge_ref[1 + 4 * i : 3 + 4 * i, :] = z[:2]
        edge_ref[3 + 4 * i : 5 + 4 * i, :] = z[T - 2 :]
        if i > 0:
            f = row_of(cst, TAPS + 3 * i) * z
            for tap in (1, 2):
                f = f + row_of(cst, TAPS + 3 * i + tap) * down(z, tap, rows)
            feat.append(f)
    u = jnp.where(rows >= 2, rnd(feat[0] * feat[1]), 0.0)
    h = scan_down(row_of(cst, KAP) * u, dec, rows)
    h_ref[...] = h
    edge_ref[0:1, :] = h[T - 1 :]
    edge_ref[13:16, :] = jnp.zeros((3, C), F32)


def fwd_out_kernel(
    near, other, z_ref, h_ref, cst, down_ref,
    gated_ref, low_ref, q_ref, k_ref, v_ref, mix_ref, next_ref, edges_ref,
):
    me = position()
    place(edges_ref, near, other)
    rows = row_ids()
    dec = row_of(cst, DEC)
    kap = row_of(cst, KAP)
    skip = row_of(cst, SKIP)
    slab = lax.broadcasted_iota(jnp.int32, (SLABS, C), 0)

    def edge(r):
        return edges_ref[:, r, :]

    def prev(v):
        return jnp.where(slab >= 1, pltpu.roll(v, 1, 0), 0.0)

    def own(v):
        return jnp.sum(jnp.where(slab == me, v, 0.0), axis=0, keepdims=True)

    def following(v):
        return jnp.sum(jnp.where(slab == me + 1, v, 0.0), axis=0, keepdims=True)

    first0, first1, full = [], [], []
    for i in range(3):
        t0, t1, t2 = (row_of(cst, TAPS + 3 * i + n) for n in range(3))
        a0, a1 = edge(1 + 4 * i), edge(2 + 4 * i)
        b0, b1 = prev(edge(3 + 4 * i)), prev(edge(4 + 4 * i))
        first0.append(t0 * a0 + t1 * b1 + t2 * b0)
        first1.append(t0 * a1 + t1 * a0 + t2 * b1)
        p0, p1 = own(b0), own(b1)
        z = z_ref[i].astype(F32)
        s1 = jnp.where(rows == 0, p1, pltpu.roll(z, 1, 0))
        s2 = jnp.where(rows == 0, p0, jnp.where(rows == 1, p1, pltpu.roll(z, 2, 0)))
        full.append(t0 * z + t1 * s1 + t2 * s2)
    u0 = rnd(first0[1] * first0[2])
    u1 = rnd(first1[1] * first1[2])
    total = edge(0) + kap * (jnp.exp(-dec * (T - 1)) * u0 + jnp.exp(-dec * (T - 2)) * u1)
    ahead = (me - 1 - slab).astype(F32)
    weight = jnp.exp(-dec * (T * jnp.maximum(ahead, 0.0)))
    carry = jnp.sum(jnp.where(slab < me, weight * total, 0.0), axis=0, keepdims=True)
    carry_next = jnp.exp(-dec * T) * carry + own(total)
    one = jnp.exp(-dec)
    power = jnp.exp(-dec * rows.astype(F32))
    bump = jnp.where(rows >= 1, kap * own(u1) * jnp.exp(dec), 0.0)
    h = h_ref[...] + power * (one * carry + kap * own(u0) + bump)
    q, kf, vf = full
    mix = rnd(h) + skip * rnd(kf * vf)
    gated = (q * mix).astype(BF16)
    gated_ref[...] = gated
    low_ref[...] = dot(gated, down_ref[...]).astype(BF16)
    q_ref[...] = q
    k_ref[...] = kf
    v_ref[...] = vf
    mix_ref[...] = mix
    n0 = following(u0)
    n1 = following(u1)
    h0 = one * carry_next + kap * n0
    h1 = one * h0 + kap * n1
    next_ref[0:1, :] = rnd(h0) + skip * n0
    next_ref[1:2, :] = rnd(h1) + skip * n1
    for i in range(3):
        next_ref[2 + 2 * i : 3 + 2 * i, :] = following(first0[i])
        next_ref[3 + 2 * i : 4 + 2 * i, :] = following(first1[i])


def part_kernel(gated_ref, low_ref, ow_ref, right_ref, left_ref, far_ref, own_ref):
    ids = block_ids()
    gated = gated_ref[...]
    for k, dst in ((3, far_ref), (2, right_ref), (1, left_ref), (0, own_ref)):
        if k > 0:
            dst[1024:1280, :] = low_ref[...]
        for r in range(4):
            cols = pl.ds(pl.multiple_of(ids[k][r] * 256, 256), 256)
            dst[r * 256 : r * 256 + 256, :] = dot(gated, ow_ref[:, cols]).astype(BF16)


def bwd_in_kernel(
    g0, g1, g2, g3, ow_ref, down_ref, q_ref, low_out, cst,
    dg_ref, gsum_ref, edge_ref, last_ref,
):
    rows = row_ids()
    dec = row_of(cst, DEC)
    ids = block_ids()
    pairs = as_pairs((g0, g1, g2, g3), 640)
    dlowd = low_sum(pairs, CUT, 256)
    last = jnp.sum(dlowd * low_out[...].astype(F32), axis=0, keepdims=True)
    last_ref[...] = jnp.broadcast_to(last, (8, RANK))
    dg = dot_nt((dlowd * row_of(cst, PICKED + 3)).astype(BF16), down_ref[...])
    for k, pair in enumerate(pairs):
        for r in range(4):
            cols = pl.ds(pl.multiple_of(ids[k][r] * 256, 256), 256)
            dg = dg + dot_nt(blk(*pair, r, 128), ow_ref[:, cols])
    dg_ref[...] = dg
    g = scan_up(row_of(cst, KAP) * rnd(dg * q_ref[...]), dec, rows)
    gsum_ref[...] = g
    edge_ref[0:2, :] = g[:2]
    edge_ref[2:4, :] = dg[:2]
    edge_ref[4:8, :] = jnp.zeros((4, C), F32)


def bwd_out_kernel(
    near, other, dg_ref, g_ref, q_ref, k_ref, v_ref, mix_ref, next_ref, cst, zraw_ref,
    zlow_ref, low_ref, rstd_ref, last_ref, up_ref, w_ref,
    right_ref, left_ref, far_ref, own_ref, rows_ref, dzb_ref, edges_ref,
):
    me = position()
    ids = block_ids()
    place(edges_ref, near, other)
    rows = row_ids()
    dec = row_of(cst, DEC)
    skip = row_of(cst, SKIP)
    slab = lax.broadcasted_iota(jnp.int32, (SLABS, C), 0)

    def following(v):
        return jnp.sum(jnp.where(slab == me + 1, v, 0.0), axis=0, keepdims=True)

    head = edges_ref[:, 0, :]
    ahead = (slab - me - 1).astype(F32)
    weight = jnp.exp(-dec * (T * jnp.maximum(ahead, 0.0)))
    carry = jnp.sum(jnp.where(slab > me, weight * head, 0.0), axis=0, keepdims=True)
    weight = jnp.exp(-dec * (T * jnp.maximum(ahead - 1.0, 0.0)))
    carry_next = jnp.sum(jnp.where(slab > me + 1, weight * head, 0.0), axis=0, keepdims=True)
    g = g_ref[...] + jnp.exp(-dec * (T - rows).astype(F32)) * carry
    dg = dg_ref[...]
    q, kf, vf = q_ref[...], k_ref[...], v_ref[...]
    dprod = rnd(g) + skip * (dg * q)
    dfeat = (dg * mix_ref[...], dprod * vf, dprod * kf)
    dg0 = following(edges_ref[:, 2, :])
    dg1 = following(edges_ref[:, 3, :])
    g1 = following(edges_ref[:, 1, :]) + jnp.exp(-dec * (T - 1)) * carry_next
    nxt = [row_of(next_ref, n) for n in range(8)]
    dp0 = rnd(carry) + skip * (dg0 * nxt[2])
    dp1 = rnd(g1) + skip * (dg1 * nxt[3])
    inside = jnp.full((1, C), me, jnp.int32) < SLABS - 1
    after0 = [jnp.where(inside, v, 0.0) for v in (dg0 * nxt[0], dp0 * nxt[6], dp0 * nxt[4])]
    after1 = [jnp.where(inside, v, 0.0) for v in (dg1 * nxt[1], dp1 * nxt[7], dp1 * nxt[5])]
    low_raw = low_ref[...]
    low_in = low_raw * rstd_ref[...]
    dlow = jnp.zeros((T, RANK), F32)
    inner = jnp.zeros((T, C), F32)
    grads = []
    for i in range(3):
        t0, t1, t2 = (row_of(cst, TAPS + 3 * i + n) for n in range(3))
        d = dfeat[i]
        s1 = jnp.where(rows == T - 1, after0[i], pltpu.roll(d, T - 1, 0))
        s2 = jnp.where(
            rows == T - 2, after0[i], jnp.where(rows == T - 1, after1[i], pltpu.roll(d, T - 2, 0))
        )
        dz = t0 * d + t1 * s1 + t2 * s2
        dzb_ref[i] = dz.astype(BF16)
        rows_ref[i : i + 1, :] = jnp.sum(dz * zlow_ref[i], axis=0, keepdims=True)
        dlowd = dot_nt((dz * row_of(cst, SCALE + i)).astype(BF16), up_ref[i])
        grads.append(jnp.sum(dlowd * low_in, axis=0, keepdims=True))
        dlow = dlow + dlowd * row_of(cst, PICKED + i)
        inner = inner + dz * zraw_ref[i]
    rows_ref[3:8, :] = jnp.zeros((5, C), F32)
    inner = line(jnp.sum(inner + dlow * low_raw, axis=1, keepdims=True))
    low = dlow.astype(BF16)
    tail = thirds(inner)
    for row in grads + [last_ref[0:1, :]]:
        tail = tail + thirds(row)
    tail = tile_of(tail)
    for k, dst in ((3, far_ref), (2, right_ref), (1, left_ref), (0, own_ref)):
        dst[1024:1280, :] = low
        dst[1280:1296, :] = tail
        for r in range(4):
            at = ids[k][r]
            acc = dot_nt(dzb_ref[0], w_ref[0, at])
            acc = acc + dot_nt(dzb_ref[1], w_ref[1, at])
            acc = acc + dot_nt(dzb_ref[2], w_ref[2, at])
            dst[r * 256 : r * 256 + 256, :] = acc.astype(BF16)


def total_of(parts, lo, hi):
    out = parts[0][lo:hi, :].astype(F32)
    for part in parts[1:]:
        out = out + part[lo:hi, :].astype(F32)
    return out


def out_sum_kernel(
    own, low_ref, rm, lm, fm, c0, c1, c2, c3, cst, near, far, gos_ref,
):
    parts = (own, rm, lm, fm)
    low = low_ref[...].astype(F32) + total_of(parts[1:], 1024, 1280)
    lowd = (low * row_of(cst, PICKED + 3)).astype(BF16)
    gos_ref[4:8, :] = jnp.zeros((4, C), F32)
    for r, z in enumerate((c0, c1, c2, c3)):
        olow = dot(lowd, z[256:512, :])
        scale = joined(z[512:528, :].astype(F32), 0)
        v = total_of(parts, r * 256, r * 256 + 256) + olow * scale
        dst = near if r < 2 else far
        dst[(r % 2) * 256 : (r % 2) * 256 + 256, :] = v.astype(BF16)
        gos_ref[r : r + 1, :] = jnp.sum(z[:256, :].astype(F32) * olow, axis=0, keepdims=True)


def out_half_kernel(near, far, keep, send):
    keep[...] = near[0:256, :].astype(F32) + far[0:256, :].astype(F32)
    send[...] = (near[256:512, :].astype(F32) + far[256:512, :].astype(F32)).astype(BF16)


def in_sum_kernel(
    own, rm, lm, fm, z0, z1, z2, z3, gos, o0, o1, o2, o3, keep,
):
    parts = (own, rm, lm, fm)
    low = total_of(parts, 1024, 1296)
    dlow = low[:256].astype(BF16)
    inner = joined(low[256:], 0)
    grads = [joined(low[256:], 3 + 3 * i) for i in range(4)]
    keep[0:1, :] = inner
    for i in range(4):
        keep[1 + i : 2 + i, :] = grads[i]
    keep[5:6, :] = gos[0:1, :]
    keep[6:8, :] = jnp.zeros((2, C), F32)
    common = []
    for row in [inner] + grads:
        common = common + thirds(row)
    for r, (z, out) in enumerate(((z0, o0), (z1, o1), (z2, o2), (z3, o3))):
        at = slice(r * 256, r * 256 + 256)
        v = total_of(parts, r * 256, r * 256 + 256)
        v = v + dot_nt(dlow, z[256:512, :])
        out[0:256, :] = v.astype(out.dtype)
        if r > 0:
            out[256:288, :] = tile_of(common + thirds(gos[r : r + 1, :]), 32)


def final_kernel(
    o0, r1, r2, r3, keep, sums, tok, cot, gain, rstd_ref, grad_ref, rows_ref,
):
    dnorm = o0[...]
    rows = [keep[i : i + 1, :] for i in range(6)]
    for ref in (r1, r2, r3):
        dnorm = dnorm + ref[0:256, :].astype(F32)
        tail = ref[256:288, :].astype(F32)
        rows = [rows[i] + joined(tail, 3 * i) for i in range(6)]
    rstd = rstd_ref[...]
    inner = column(rows[0]) * (rstd * rstd * rstd / WIDTH)
    x = tok[...].astype(F32)
    grad = cot[...].astype(F32) + rstd * (gain[...].astype(F32) * dnorm) - x * inner
    grad_ref[...] = grad.astype(BF16)
    rows_ref[0:3, :] = sums[0:3, :]
    rows_ref[3:4, :] = rows[5]
    for i in range(4):
        rows_ref[4 + i : 5 + i, :] = rows[1 + i]


def table_kernel(pick, rep, table_ref, gis_ref, gos_ref):
    rows = rep[0]
    for i in range(1, SLABS):
        rows = rows + rep[i]
    gis_ref[...] = rows[0:3]
    gos_ref[...] = rows[3:4]
    for g in range(4):
        out = jnp.zeros((1, RANK), F32)
        for i in range(4):
            chosen = jnp.full((1, RANK), pick[i], jnp.int32) == g
            out = out + jnp.where(chosen, rows[4 + i : 5 + i], 0.0)
        table_ref[g : g + 1, :] = out


VMEM = pl.BlockSpec(memory_space=pltpu.VMEM)
SMEM = pl.BlockSpec(memory_space=pltpu.SMEM)


def call(kernel, outs, args, scalars=False, scratch=(), flops=1 << 24, after=(), hold=()):
    specs = [VMEM] * len(args)
    if scalars:
        specs[0] = SMEM
    body = kernel
    if after or hold:
        n, m = len(args), len(after) + len(hold)

        def body(*refs):
            kernel(*refs[:n], *refs[n + m :])

        specs = specs + [VMEM] * len(hold) + [pl.BlockSpec(memory_space=pl.ANY)] * len(after)
        args = list(args) + list(hold) + list(after)
    outs = [jax.ShapeDtypeStruct(s, d) for s, d in outs]
    size = sum(v.size * v.dtype.itemsize for v in list(args) + outs)
    return pl.pallas_call(
        body,
        out_shape=outs,
        in_specs=specs,
        out_specs=[VMEM] * len(outs),
        scratch_shapes=list(scratch),
        compiler_params=pltpu.CompilerParams(vmem_limit_bytes=16 * 2**20),
        cost_estimate=pl.CostEstimate(flops=flops, bytes_accessed=size, transcendentals=0),
    )(*args)


def on_device(
    tokens,
    cotangent,
    norm_gain,
    in_weight,
    in_down,
    in_up,
    in_scale,
    scale_table,
    table_pick,
    short_taps,
    residue,
    decay,
    skip_gain,
    out_weight,
    out_down,
    out_up,
    out_scale,
):
    kap = residue * jnp.sqrt(-jnp.expm1(-2.0 * decay))
    weight = jnp.transpose(in_weight, (1, 0, 2)).reshape(3, 16, 256, C)
    up_in = jnp.transpose(in_up, (1, 0, 2))
    gain = norm_gain[None]
    (cst,) = call(
        const_kernel,
        [((24, C), F32)],
        [table_pick, kap[None], decay[None], skip_gain[None], in_scale, short_taps, scale_table],
        scalars=True,
        hold=[weight, up_in],
    )
    tz0 = jnp.concatenate([tokens, in_down, gain, jnp.zeros((15, C), BF16)], 0)
    tz = [tz0] + [across(tz0, "zh", r) for r in (1, 2, 3)]
    (cz0,) = call(
        cot_start_kernel, [((528, C), BF16)], [cotangent, out_up, out_scale[None], tz[2]]
    )
    cz = [cz0] + [across(cz0, "zh", r) for r in (1, 2, 3)]
    (pay,) = call(token_kernel, [((1296, C), BF16)], tz, after=[cst])
    tr = ring_gather(pay, 656)
    (cpay,) = call(cot_kernel, [((1280, C), BF16)], cz)
    cr = x_gather(cpay)
    zraw, z, zlow, h, edge, low_raw, rstd = call(
        fwd_in_kernel,
        [((3, T, C), F32), ((3, T, C), BF16), ((3, T, C), F32), ((T, C), F32), ((16, C), F32),
         ((T, RANK), F32), ((T, 1), F32)],
        [*tr, weight, up_in, cst],
        after=[cpay],
        flops=2 * T * WIDTH * 3 * C,
    )
    edges, _ = ctx_gather(edge)
    gated, low_out, q, kf, vf, mix, nxt = call(
        fwd_out_kernel,
        [((T, C), BF16)] * 2 + [((T, C), F32)] * 4 + [((8, C), F32)],
        [*edges, z, h, cst, out_down],
        scratch=[pltpu.VMEM((SLABS, 16, C), F32)],
    )
    *out, own_out = call(
        part_kernel,
        [((1280, C), BF16)] * 3 + [((1024, C), BF16)],
        [gated, low_out, out_weight],
        flops=2 * T * WIDTH * C,
    )
    got_out = x_scatter(*out)
    dg, gsum, gedge, last = call(
        bwd_in_kernel,
        [((T, C), F32), ((T, C), F32), ((8, C), F32), ((8, RANK), F32)],
        [*cr, out_weight, out_down, q, low_out, cst],
        after=[own_out],
        flops=2 * T * WIDTH * C,
    )
    gedges, _ = ctx_gather(gedge)
    *out, own, sums = call(
        bwd_out_kernel,
        [((1296, C), BF16)] * 4 + [((8, C), F32)],
        [*gedges, dg, gsum, q, kf, vf, mix, nxt, cst, zraw, zlow, low_raw, rstd, last, up_in,
         weight],
        scratch=[pltpu.VMEM((3, T, C), BF16), pltpu.VMEM((SLABS, 8, C), F32)],
        flops=2 * T * WIDTH * 3 * C,
    )
    got = x_scatter(*out)
    half = [((512, C), BF16)] * 2
    near, far_out, gos = call(
        out_sum_kernel, half + [((8, C), F32)], [own_out, low_out, *got_out, *cz, cst], after=[sums]
    )
    keep, send = call(
        out_half_kernel, [((T, C), F32), ((T, C), BF16)], [near, across(far_out, "zh", 2)]
    )
    mixed = tokens.astype(F32) + keep + across(send, "zh", 1).astype(F32)
    mixed = mixed.astype(BF16)

    payload = [((T, C), F32)] + [((288, C), BF16)] * 3 + [((8, C), F32)]
    o0, o1, o2, o3, inner = call(
        in_sum_kernel, payload, [own, *got, *tz, gos], after=[mixed]
    )
    got = [across(o, "zh", r) for r, o in ((1, o1), (2, o2), (3, o3))]
    grad_tokens, rows = call(
        final_kernel,
        [((T, C), BF16), ((8, C), F32)],
        [o0, *got, inner, sums, tokens, cotangent, gain, rstd],
    )
    grad_table, grad_in_scale, grad_out_scale = call(
        table_kernel,
        [((4, RANK), F32), ((3, C), F32), ((1, C), F32)],
        [table_pick, ctx_spread(rows)],
        scalars=True,
    )
    return (mixed, grad_tokens, grad_table, grad_in_scale, grad_out_scale[0])


def solution(mesh):
    fine = Mesh(mesh.devices.reshape(2, 4, 2, 4, 4), CTX + TP)
    return jax.shard_map(
        on_device,
        mesh=fine,
        in_specs=(
            P(CTX, TP),
            P(CTX, TP),
            P(TP),
            P(None, None, TP),
            P(TP, None),
            P(None, None, TP),
            P(None, TP),
            P(),
            P(),
            P(None, None, TP),
            P(TP),
            P(TP),
            P(TP),
            P(TP, None),
            P(TP, None),
            P(None, TP),
            P(TP),
        ),
        out_specs=(P(CTX, TP), P(CTX, TP), P(), P(None, TP), P(TP)),
        check_vma=False,
    )
```

profile of v0, /device:TPU:1, one launch (start us, length us, event | category | flops | bytes accessed | tf_op | source)
XLA Modules:
  0.0 191.3 jit_solution(12690637838974380731)
XLA Ops:
  2.6 6.9 %collective-permute-start.2 = (bf16[528,256]{1,0:T(8,128)(2,1)S(1)}, bf16[528,256]{1,0:T(8,128)(2,1)S(1)}, u32[]{:S(2)}, u32[]{:S(2)}) collective-permute-start(bf16[528,256]{1,0:T(8,128)(2,1)S(1)} %maximum_maximum_fusion.refs_0_.refs_4_), channel_id=1, source_target_pairs={{0,3},{1,2},{2,1},{3,0},{4,7},{5,6},{6,5},{7,4},{8,11},{9,10},{10,... | collective-permute-start | bytes 811016 | tf_op jit(solution)/shard_map/ppermute | solution.py:48
  12.4 2.8 %copy-done = bf16[4096,3,256]{2,0,1:T(8,128)(2,1)S(1)} copy-done((bf16[4096,3,256]{2,0,1:T(8,128)(2,1)S(1)}, bf16[4096,3,256]{2,0,1:T(8,128)(2,1)}, u32[]{:S(2)}) %copy-start) | copy-done | bytes 6291480
  20.9 11.8 %collective-permute-done.2.refs_3_.refs_7_ = bf16[528,256]{1,0:T(8,128)(2,1)S(1)} collective-permute-done((bf16[528,256]{1,0:T(8,128)(2,1)S(1)}, bf16[528,256]{1,0:T(8,128)(2,1)S(1)}, u32[]{:S(2)}, u32[]{:S(2)}) %collective-permute-start.2) | collective-permute-done | bytes 270368 | tf_op jit(solution)/shard_map/ppermute | solution.py:48
  32.7 3.8 %collective-permute-done.refs_1_.refs_5_ = bf16[528,256]{1,0:T(8,128)(2,1)S(1)} collective-permute-done((bf16[528,256]{1,0:T(8,128)(2,1)S(1)}, bf16[528,256]{1,0:T(8,128)(2,1)S(1)}, u32[]{:S(2)}, u32[]{:S(2)}) %collective-permute-start) | collective-permute-done | bytes 270368 | tf_op jit(solution)/shard_map/ppermute | solution.py:48
  41.0 3.1 %collective-permute-start.8 = (bf16[528,256]{1,0:T(8,128)(2,1)S(1)}, bf16[528,256]{1,0:T(8,128)(2,1)S(1)}, u32[]{:S(2)}, u32[]{:S(2)}) collective-permute-start(bf16[528,256]{1,0:T(8,128)(2,1)S(1)} %shard_map.203.z0.refs_5_), channel_id=1, source_target_pairs={{0,2},{1,3},{2,0},{3,1},{4,6},{5,7},{6,4},{7,5},{8,10},{9,11},{10,... | collective-permute-start | bytes 811016 | tf_op jit(solution)/shard_map/ppermute | solution.py:48
  45.2 8.0 %collective-permute-done.4.right_ref.refs_2_ = bf16[1296,256]{1,0:T(8,128)(2,1)S(1)} collective-permute-done((bf16[1296,256]{1,0:T(8,128)(2,1)S(1)}, bf16[1296,256]{1,0:T(8,128)(2,1)S(1)}, u32[]{:S(2)}, u32[]{:S(2)}) %collective-permute-start.4) | collective-permute-done | bytes 663584 | tf_op jit(solution)/shard_map/ppermute | solution.py:25
  53.2 3.1 %collective-permute-done.3.left_ref.refs_1_ = bf16[1296,256]{1,0:T(8,128)(2,1)S(1)} collective-permute-done((bf16[1296,256]{1,0:T(8,128)(2,1)S(1)}, bf16[1296,256]{1,0:T(8,128)(2,1)S(1)}, u32[]{:S(2)}, u32[]{:S(2)}) %collective-permute-start.3) | collective-permute-done | bytes 663584 | tf_op jit(solution)/shard_map/ppermute | solution.py:25
  56.4 2.7 %collective-permute-start.6 = (bf16[640,256]{1,0:T(8,128)(2,1)S(1)}, bf16[640,256]{1,0:T(8,128)(2,1)S(1)}, u32[]{:S(2)}, u32[]{:S(2)}) collective-permute-start(bf16[640,256]{1,0:T(8,128)(2,1)S(1)} %get-tuple-element.50), channel_id=1, source_target_pairs={{0,12},{4,0},{8,4},{12,8},{1,13},{5,1},{9,5},{13,9},{2,14},{6,2},{... | collective-permute-start | bytes 983048 | tf_op jit(solution)/shard_map/ppermute | solution.py:25
  59.1 3.0 %collective-permute-done.9.z3.refs_8_ = bf16[528,256]{1,0:T(8,128)(2,1)S(1)} collective-permute-done((bf16[528,256]{1,0:T(8,128)(2,1)S(1)}, bf16[528,256]{1,0:T(8,128)(2,1)S(1)}, u32[]{:S(2)}, u32[]{:S(2)}) %collective-permute-start.9) | collective-permute-done | bytes 270368 | tf_op jit(solution)/shard_map/ppermute | solution.py:48
  62.1 7.9 %collective-permute-done.7.z1.refs_6_ = bf16[528,256]{1,0:T(8,128)(2,1)S(1)} collective-permute-done((bf16[528,256]{1,0:T(8,128)(2,1)S(1)}, bf16[528,256]{1,0:T(8,128)(2,1)S(1)}, u32[]{:S(2)}, u32[]{:S(2)}) %collective-permute-start.7) | collective-permute-done | bytes 270368 | tf_op jit(solution)/shard_map/ppermute | solution.py:48
  81.3 2.9 %collective-permute-start.12 = (f32[2,2,16,256]{3,2,1,0:T(8,128)S(1)}, f32[2,2,16,256]{3,2,1,0:T(8,128)S(1)}, u32[]{:S(2)}, u32[]{:S(2)}) collective-permute-start(f32[2,2,16,256]{3,2,1,0:T(8,128)S(1)} %shard_map.207.refs_0_), channel_id=1, source_target_pairs={{0,64},{32,96},{64,0},{96,32},{1,65},{33,97},{65,1},{97,33},{2,66}... | collective-permute-start | bytes 196616 | tf_op jit(solution)/shard_map/ppermute | solution.py:48
  86.4 4.1 %collective-permute-done.13.other = f32[2,2,2,16,256]{4,3,2,1,0:T(8,128)S(1)} collective-permute-done((f32[2,2,2,16,256]{4,3,2,1,0:T(8,128)S(1)}, f32[2,2,2,16,256]{4,3,2,1,0:T(8,128)S(1)}, u32[]{:S(2)}, u32[]{:S(2)}) %collective-permute-start.13) | collective-permute-done | bytes 131104 | tf_op jit(solution)/shard_map/ppermute | solution.py:29
  95.3 6.9 %collective-permute-done.18.refs_2_ = bf16[1280,256]{1,0:T(8,128)(2,1)S(1)} collective-permute-done((bf16[1280,256]{1,0:T(8,128)(2,1)S(1)}, bf16[1280,256]{1,0:T(8,128)(2,1)S(1)}, u32[]{:S(2)}, u32[]{:S(2)}) %collective-permute-start.18) | collective-permute-done | bytes 655392 | tf_op jit(solution)/shard_map/ppermute | solution.py:25
  109.3 2.9 %collective-permute-start.22 = (f32[2,2,8,256]{3,2,1,0:T(8,128)S(1)}, f32[2,2,8,256]{3,2,1,0:T(8,128)S(1)}, u32[]{:S(2)}, u32[]{:S(2)}) collective-permute-start(f32[2,2,8,256]{3,2,1,0:T(8,128)S(1)} %shard_map.213.refs_0_), channel_id=1, source_target_pairs={{0,64},{32,96},{64,0},{96,32},{1,65},{33,97},{65,1},{97,33},{2,66}... | collective-permute-start | bytes 98312 | tf_op jit(solution)/shard_map/ppermute | solution.py:48
  113.6 3.4 %collective-permute-done.23.other = f32[2,2,2,8,256]{4,3,2,1,0:T(8,128)S(1)} collective-permute-done((f32[2,2,2,8,256]{4,3,2,1,0:T(8,128)S(1)}, f32[2,2,2,8,256]{4,3,2,1,0:T(8,128)S(1)}, u32[]{:S(2)}, u32[]{:S(2)}) %collective-permute-start.23) | collective-permute-done | bytes 65568 | tf_op jit(solution)/shard_map/ppermute | solution.py:29
  119.5 2.7 %collective-permute-start.27 = (bf16[1296,256]{1,0:T(8,128)(2,1)S(1)}, bf16[1296,256]{1,0:T(8,128)(2,1)S(1)}, u32[]{:S(2)}, u32[]{:S(2)}) collective-permute-start(bf16[1296,256]{1,0:T(8,128)(2,1)S(1)} %get-tuple-element.80), channel_id=1, source_target_pairs={{0,12},{4,0},{8,4},{12,8},{1,13},{5,1},{9,5},{13,9},{2,14},{6,2},{... | collective-permute-start | bytes 1990664 | tf_op jit(solution)/shard_map/ppermute | solution.py:25
  122.1 7.8 %collective-permute-done.16.refs_4_ = bf16[1280,256]{1,0:T(8,128)(2,1)S(1)} collective-permute-done((bf16[1280,256]{1,0:T(8,128)(2,1)S(1)}, bf16[1280,256]{1,0:T(8,128)(2,1)S(1)}, u32[]{:S(2)}, u32[]{:S(2)}) %collective-permute-start.16) | collective-permute-done | bytes 655392 | tf_op jit(solution)/shard_map/ppermute | solution.py:25
  130.6 3.4 %collective-permute-start.24 = (bf16[512,256]{1,0:T(8,128)(2,1)S(1)}, bf16[512,256]{1,0:T(8,128)(2,1)S(1)}, u32[]{:S(2)}, u32[]{:S(2)}) collective-permute-start(bf16[512,256]{1,0:T(8,128)(2,1)S(1)} %get-tuple-element.75), channel_id=1, source_target_pairs={{0,2},{1,3},{2,0},{3,1},{4,6},{5,7},{6,4},{7,5},{8,10},{9,11},{10,... | collective-permute-start | bytes 786440 | tf_op jit(solution)/shard_map/ppermute | solution.py:48
  133.9 14.3 %collective-permute-done.24.far = bf16[512,256]{1,0:T(8,128)(2,1)S(1)} collective-permute-done((bf16[512,256]{1,0:T(8,128)(2,1)S(1)}, bf16[512,256]{1,0:T(8,128)(2,1)S(1)}, u32[]{:S(2)}, u32[]{:S(2)}) %collective-permute-start.24) | collective-permute-done | bytes 262176 | tf_op jit(solution)/shard_map/ppermute | solution.py:48
  148.4 8.3 %collective-permute-done.25 = bf16[256,256]{1,0:T(8,128)(2,1)S(1)} collective-permute-done((bf16[256,256]{1,0:T(8,128)(2,1)S(1)}, bf16[256,256]{1,0:T(8,128)(2,1)S(1)}, u32[]{:S(2)}, u32[]{:S(2)}) %collective-permute-start.25) | collective-permute-done | bytes 131104 | tf_op jit(solution)/shard_map/ppermute | solution.py:48
  159.0 3.4 %collective-permute-start.30 = (bf16[288,256]{1,0:T(8,128)(2,1)S(1)}, bf16[288,256]{1,0:T(8,128)(2,1)S(1)}, u32[]{:S(2)}, u32[]{:S(2)}) collective-permute-start(bf16[288,256]{1,0:T(8,128)(2,1)S(1)} %get-tuple-element.85), channel_id=1, source_target_pairs={{0,2},{1,3},{2,0},{3,1},{4,6},{5,7},{6,4},{7,5},{8,10},{9,11},{10,... | collective-permute-start | bytes 442376 | tf_op jit(solution)/shard_map/ppermute | solution.py:48
  164.6 7.4 %collective-permute-done.29.r1 = bf16[288,256]{1,0:T(8,128)(2,1)S(1)} collective-permute-done((bf16[288,256]{1,0:T(8,128)(2,1)S(1)}, bf16[288,256]{1,0:T(8,128)(2,1)S(1)}, u32[]{:S(2)}, u32[]{:S(2)}) %collective-permute-start.29) | collective-permute-done | bytes 147488 | tf_op jit(solution)/shard_map/ppermute | solution.py:48
  172.1 5.1 %collective-permute-done.31.r3 = bf16[288,256]{1,0:T(8,128)(2,1)S(1)} collective-permute-done((bf16[288,256]{1,0:T(8,128)(2,1)S(1)}, bf16[288,256]{1,0:T(8,128)(2,1)S(1)}, u32[]{:S(2)}, u32[]{:S(2)}) %collective-permute-start.31) | collective-permute-done | bytes 147488 | tf_op jit(solution)/shard_map/ppermute | solution.py:48
  178.1 12.0 %all_to_all.5.rep = f32[16,8,256]{2,1,0:T(8,128)S(1)} all-to-all(f32[16,8,256]{2,1,0:T(8,128)S(1)} %broadcast_in_dim.30), channel_id=1, replica_groups=mesh['zl'=2,'y'=4,'core'=2,'x'=4,'zh'=4] {'zl','y','core'}, dimensions={0} | all-to-all | bytes 262144 | tf_op jit(solution)/shard_map/all_to_all | solution.py:53
  (105 shorter events, 52.7 us)
Async XLA Ops:
  2.6 30.1 %collective-permute-start.2 = (bf16[528,256]{1,0:T(8,128)(2,1)S(1)}, bf16[528,256]{1,0:T(8,128)(2,1)S(1)}, u32[]{:S(2)}, u32[]{:S(2)}) collective-permute-start(bf16[528,256]{1,0:T(8,128)(2,1)S(1)} %maximum_maximum_fusion.refs_0_.refs_4_), channel_id=1, source_target_pairs={{0,3},{1,2},{2,1},{3,0},{4,7},{5,6},{6,5},{7,4},{8,11},{9,10},{10,... | collective-permute-start | bytes 811016 | tf_op jit(solution)/shard_map/ppermute | solution.py:48
  9.5 23.2 %collective-permute-start.1 = (bf16[528,256]{1,0:T(8,128)(2,1)S(1)}, bf16[528,256]{1,0:T(8,128)(2,1)S(1)}, u32[]{:S(2)}, u32[]{:S(2)}) collective-permute-start(bf16[528,256]{1,0:T(8,128)(2,1)S(1)} %maximum_maximum_fusion.refs_0_.refs_4_), channel_id=1, source_target_pairs={{0,2},{1,3},{2,0},{3,1},{4,6},{5,7},{6,4},{7,5},{8,10},{9,11},{10,... | collective-permute-start | bytes 811016 | tf_op jit(solution)/shard_map/ppermute | solution.py:48
  10.5 26.0 %collective-permute-start = (bf16[528,256]{1,0:T(8,128)(2,1)S(1)}, bf16[528,256]{1,0:T(8,128)(2,1)S(1)}, u32[]{:S(2)}, u32[]{:S(2)}) collective-permute-start(bf16[528,256]{1,0:T(8,128)(2,1)S(1)} %maximum_maximum_fusion.refs_0_.refs_4_), channel_id=1, source_target_pairs={{0,1},{1,0},{2,3},{3,2},{4,5},{5,4},{6,7},{7,6},{8,9},{9,8},{10,11... | collective-permute-start | bytes 811016 | tf_op jit(solution)/shard_map/ppermute | solution.py:48
  36.9 16.3 %collective-permute-start.4 = (bf16[1296,256]{1,0:T(8,128)(2,1)S(1)}, bf16[1296,256]{1,0:T(8,128)(2,1)S(1)}, u32[]{:S(2)}, u32[]{:S(2)}) collective-permute-start(bf16[1296,256]{1,0:T(8,128)(2,1)S(1)} %shard_map.201.refs_0_), channel_id=1, source_target_pairs={{0,12},{4,0},{8,4},{12,8},{1,13},{5,1},{9,5},{13,9},{2,14},{6,2},{... | collective-permute-start | bytes 1990664 | tf_op jit(solution)/shard_map/ppermute | solution.py:25
  39.4 16.9 %collective-permute-start.3 = (bf16[1296,256]{1,0:T(8,128)(2,1)S(1)}, bf16[1296,256]{1,0:T(8,128)(2,1)S(1)}, u32[]{:S(2)}, u32[]{:S(2)}) collective-permute-start(bf16[1296,256]{1,0:T(8,128)(2,1)S(1)} %shard_map.201.refs_0_), channel_id=1, source_target_pairs={{0,4},{4,8},{8,12},{12,0},{1,5},{5,9},{9,13},{13,1},{2,6},{6,10},{... | collective-permute-start | bytes 1990664 | tf_op jit(solution)/shard_map/ppermute | solution.py:25
  39.5 22.6 %collective-permute-start.9 = (bf16[528,256]{1,0:T(8,128)(2,1)S(1)}, bf16[528,256]{1,0:T(8,128)(2,1)S(1)}, u32[]{:S(2)}, u32[]{:S(2)}) collective-permute-start(bf16[528,256]{1,0:T(8,128)(2,1)S(1)} %shard_map.203.z0.refs_5_), channel_id=1, source_target_pairs={{0,3},{1,2},{2,1},{3,0},{4,7},{5,6},{6,5},{7,4},{8,11},{9,10},{10,... | collective-permute-start | bytes 811016 | tf_op jit(solution)/shard_map/ppermute | solution.py:48
  41.0 21.1 %collective-permute-start.8 = (bf16[528,256]{1,0:T(8,128)(2,1)S(1)}, bf16[528,256]{1,0:T(8,128)(2,1)S(1)}, u32[]{:S(2)}, u32[]{:S(2)}) collective-permute-start(bf16[528,256]{1,0:T(8,128)(2,1)S(1)} %shard_map.203.z0.refs_5_), channel_id=1, source_target_pairs={{0,2},{1,3},{2,0},{3,1},{4,6},{5,7},{6,4},{7,5},{8,10},{9,11},{10,... | collective-permute-start | bytes 811016 | tf_op jit(solution)/shard_map/ppermute | solution.py:48
  44.0 26.0 %collective-permute-start.7 = (bf16[528,256]{1,0:T(8,128)(2,1)S(1)}, bf16[528,256]{1,0:T(8,128)(2,1)S(1)}, u32[]{:S(2)}, u32[]{:S(2)}) collective-permute-start(bf16[528,256]{1,0:T(8,128)(2,1)S(1)} %shard_map.203.z0.refs_5_), channel_id=1, source_target_pairs={{0,1},{1,0},{2,3},{3,2},{4,5},{5,4},{6,7},{7,6},{8,9},{9,8},{10,11... | collective-permute-start | bytes 811016 | tf_op jit(solution)/shard_map/ppermute | solution.py:48
  56.3 17.4 %collective-permute-start.5 = (bf16[656,256]{1,0:T(8,128)(2,1)S(1)}, bf16[656,256]{1,0:T(8,128)(2,1)S(1)}, u32[]{:S(2)}, u32[]{:S(2)}) collective-permute-start(bf16[656,256]{1,0:T(8,128)(2,1)S(1)} %get-tuple-element.49), channel_id=1, source_target_pairs={{0,4},{4,8},{8,12},{12,0},{1,5},{5,9},{9,13},{13,1},{2,6},{6,10},{... | collective-permute-start | bytes 1007624 | tf_op jit(solution)/shard_map/ppermute | solution.py:25
  56.4 17.3 %collective-permute-start.6 = (bf16[640,256]{1,0:T(8,128)(2,1)S(1)}, bf16[640,256]{1,0:T(8,128)(2,1)S(1)}, u32[]{:S(2)}, u32[]{:S(2)}) collective-permute-start(bf16[640,256]{1,0:T(8,128)(2,1)S(1)} %get-tuple-element.50), channel_id=1, source_target_pairs={{0,12},{4,0},{8,4},{12,8},{1,13},{5,1},{9,5},{13,9},{2,14},{6,2},{... | collective-permute-start | bytes 983048 | tf_op jit(solution)/shard_map/ppermute | solution.py:25
  70.4 24.3 %collective-permute-start.19 = (bf16[1280,256]{1,0:T(8,128)(2,1)S(1)}, bf16[1280,256]{1,0:T(8,128)(2,1)S(1)}, u32[]{:S(2)}, u32[]{:S(2)}) collective-permute-start(bf16[1280,256]{1,0:T(8,128)(2,1)S(1)} %shard_map.204.refs_8_.refs_0_), channel_id=1, source_target_pairs={{0,8},{4,12},{8,0},{12,4},{1,9},{5,13},{9,1},{13,5},{2,10},{6,14},... | collective-permute-start | bytes 1966088 | tf_op jit(solution)/shard_map/ppermute | solution.py:25
  72.2 30.0 %collective-permute-start.18 = (bf16[1280,256]{1,0:T(8,128)(2,1)S(1)}, bf16[1280,256]{1,0:T(8,128)(2,1)S(1)}, u32[]{:S(2)}, u32[]{:S(2)}) collective-permute-start(bf16[1280,256]{1,0:T(8,128)(2,1)S(1)} %shard_map.204.refs_8_.refs_0_), channel_id=1, source_target_pairs={{0,12},{4,0},{8,4},{12,8},{1,13},{5,1},{9,5},{13,9},{2,14},{6,2},{... | collective-permute-start | bytes 1966088 | tf_op jit(solution)/shard_map/ppermute | solution.py:25
  73.2 29.4 %collective-permute-start.17 = (bf16[1280,256]{1,0:T(8,128)(2,1)S(1)}, bf16[1280,256]{1,0:T(8,128)(2,1)S(1)}, u32[]{:S(2)}, u32[]{:S(2)}) collective-permute-start(bf16[1280,256]{1,0:T(8,128)(2,1)S(1)} %shard_map.204.refs_8_.refs_0_), channel_id=1, source_target_pairs={{0,4},{4,8},{8,12},{12,0},{1,5},{5,9},{9,13},{13,1},{2,6},{6,10},{... | collective-permute-start | bytes 1966088 | tf_op jit(solution)/shard_map/ppermute | solution.py:25
  91.9 30.2 %collective-permute-start.14 = (bf16[1280,256]{1,0:T(8,128)(2,1)S(1)}, bf16[1280,256]{1,0:T(8,128)(2,1)S(1)}, u32[]{:S(2)}, u32[]{:S(2)}) collective-permute-start(bf16[1280,256]{1,0:T(8,128)(2,1)S(1)} %get-tuple-element.57), channel_id=1, source_target_pairs={{0,4},{4,8},{8,12},{12,0},{1,5},{5,9},{9,13},{13,1},{2,6},{6,10},{... | collective-permute-start | bytes 1966088 | tf_op jit(solution)/shard_map/ppermute | solution.py:25
  93.2 28.9 %collective-permute-start.15 = (bf16[1280,256]{1,0:T(8,128)(2,1)S(1)}, bf16[1280,256]{1,0:T(8,128)(2,1)S(1)}, u32[]{:S(2)}, u32[]{:S(2)}) collective-permute-start(bf16[1280,256]{1,0:T(8,128)(2,1)S(1)} %get-tuple-element.58), channel_id=1, source_target_pairs={{0,12},{4,0},{8,4},{12,8},{1,13},{5,1},{9,5},{13,9},{2,14},{6,2},{... | collective-permute-start | bytes 1966088 | tf_op jit(solution)/shard_map/ppermute | solution.py:25
  94.7 35.3 %collective-permute-start.16 = (bf16[1280,256]{1,0:T(8,128)(2,1)S(1)}, bf16[1280,256]{1,0:T(8,128)(2,1)S(1)}, u32[]{:S(2)}, u32[]{:S(2)}) collective-permute-start(bf16[1280,256]{1,0:T(8,128)(2,1)S(1)} %get-tuple-element.59), channel_id=1, source_target_pairs={{0,8},{4,12},{8,0},{12,4},{1,9},{5,13},{9,1},{13,5},{2,10},{6,14},... | collective-permute-start | bytes 1966088 | tf_op jit(solution)/shard_map/ppermute | solution.py:25
  119.4 37.4 %collective-permute-start.26 = (bf16[1296,256]{1,0:T(8,128)(2,1)S(1)}, bf16[1296,256]{1,0:T(8,128)(2,1)S(1)}, u32[]{:S(2)}, u32[]{:S(2)}) collective-permute-start(bf16[1296,256]{1,0:T(8,128)(2,1)S(1)} %get-tuple-element.79), channel_id=1, source_target_pairs={{0,4},{4,8},{8,12},{12,0},{1,5},{5,9},{9,13},{13,1},{2,6},{6,10},{... | collective-permute-start | bytes 1990664 | tf_op jit(solution)/shard_map/ppermute | solution.py:25
  119.5 37.3 %collective-permute-start.27 = (bf16[1296,256]{1,0:T(8,128)(2,1)S(1)}, bf16[1296,256]{1,0:T(8,128)(2,1)S(1)}, u32[]{:S(2)}, u32[]{:S(2)}) collective-permute-start(bf16[1296,256]{1,0:T(8,128)(2,1)S(1)} %get-tuple-element.80), channel_id=1, source_target_pairs={{0,12},{4,0},{8,4},{12,8},{1,13},{5,1},{9,5},{13,9},{2,14},{6,2},{... | collective-permute-start | bytes 1990664 | tf_op jit(solution)/shard_map/ppermute | solution.py:25
  122.1 36.3 %collective-permute-start.28 = (bf16[1296,256]{1,0:T(8,128)(2,1)S(1)}, bf16[1296,256]{1,0:T(8,128)(2,1)S(1)}, u32[]{:S(2)}, u32[]{:S(2)}) collective-permute-start(bf16[1296,256]{1,0:T(8,128)(2,1)S(1)} %get-tuple-element.81), channel_id=1, source_target_pairs={{0,8},{4,12},{8,0},{12,4},{1,9},{5,13},{9,1},{13,5},{2,10},{6,14},... | collective-permute-start | bytes 1990664 | tf_op jit(solution)/shard_map/ppermute | solution.py:25
  130.6 17.6 %collective-permute-start.24 = (bf16[512,256]{1,0:T(8,128)(2,1)S(1)}, bf16[512,256]{1,0:T(8,128)(2,1)S(1)}, u32[]{:S(2)}, u32[]{:S(2)}) collective-permute-start(bf16[512,256]{1,0:T(8,128)(2,1)S(1)} %get-tuple-element.75), channel_id=1, source_target_pairs={{0,2},{1,3},{2,0},{3,1},{4,6},{5,7},{6,4},{7,5},{8,10},{9,11},{10,... | collective-permute-start | bytes 786440 | tf_op jit(solution)/shard_map/ppermute | solution.py:48
  148.3 8.4 %collective-permute-start.25 = (bf16[256,256]{1,0:T(8,128)(2,1)S(1)}, bf16[256,256]{1,0:T(8,128)(2,1)S(1)}, u32[]{:S(2)}, u32[]{:S(2)}) collective-permute-start(bf16[256,256]{1,0:T(8,128)(2,1)S(1)} %get-tuple-element.77), channel_id=1, source_target_pairs={{0,1},{1,0},{2,3},{3,2},{4,5},{5,4},{6,7},{7,6},{8,9},{9,8},{10,11... | collective-permute-start | bytes 393224 | tf_op jit(solution)/shard_map/ppermute | solution.py:48
  158.9 13.2 %collective-permute-start.29 = (bf16[288,256]{1,0:T(8,128)(2,1)S(1)}, bf16[288,256]{1,0:T(8,128)(2,1)S(1)}, u32[]{:S(2)}, u32[]{:S(2)}) collective-permute-start(bf16[288,256]{1,0:T(8,128)(2,1)S(1)} %get-tuple-element.84), channel_id=1, source_target_pairs={{0,1},{1,0},{2,3},{3,2},{4,5},{5,4},{6,7},{7,6},{8,9},{9,8},{10,11... | collective-permute-start | bytes 442376 | tf_op jit(solution)/shard_map/ppermute | solution.py:48
  159.0 13.1 %collective-permute-start.30 = (bf16[288,256]{1,0:T(8,128)(2,1)S(1)}, bf16[288,256]{1,0:T(8,128)(2,1)S(1)}, u32[]{:S(2)}, u32[]{:S(2)}) collective-permute-start(bf16[288,256]{1,0:T(8,128)(2,1)S(1)} %get-tuple-element.85), channel_id=1, source_target_pairs={{0,2},{1,3},{2,0},{3,1},{4,6},{5,7},{6,4},{7,5},{8,10},{9,11},{10,... | collective-permute-start | bytes 442376 | tf_op jit(solution)/shard_map/ppermute | solution.py:48
  162.4 14.8 %collective-permute-start.31 = (bf16[288,256]{1,0:T(8,128)(2,1)S(1)}, bf16[288,256]{1,0:T(8,128)(2,1)S(1)}, u32[]{:S(2)}, u32[]{:S(2)}) collective-permute-start(bf16[288,256]{1,0:T(8,128)(2,1)S(1)} %get-tuple-element.86), channel_id=1, source_target_pairs={{0,3},{1,2},{2,1},{3,0},{4,7},{5,6},{6,5},{7,4},{8,11},{9,10},{10,... | collective-permute-start | bytes 442376 | tf_op jit(solution)/shard_map/ppermute | solution.py:48
  (26 other events, 471.9 us)
where the time goes:
time: 192 us; the launch traced here: 191 us
  waiting for transfers between devices  106 us (55%)
  starting transfers between devices  50.5 us (26%)
  blocking collectives  12 us (6%)
  Pallas kernels  11.7 us (6%)
  local copies, waits for them, and re-layouts  8.7 us (5%)
    ppermute x15, waiting for transfers between devices, across(): return lax.ppermute(v, axis, [(i, i ^ bit) for i in range(4)])  68.4 us
    ppermute x15, starting transfers between devices, across(): return lax.ppermute(v, axis, [(i, i ^ bit) for i in range(4)])  32.5 us
    ppermute x13, waiting for transfers between devices, shift(): return lax.ppermute(v, axis, [(i, (i + k) % 4) for i in range(4)])  28 us
    ppermute x13, starting transfers between devices, shift(): return lax.ppermute(v, axis, [(i, (i + k) % 4) for i in range(4)])  14.7 us
    all_to_all x1, blocking collectives, ctx_spread(): return lax.all_to_all(wide, CTX, split_axis=0, concat_axis=0, tiled=True)  12 us
    pallas_call x21, Pallas kernels, call(): pl.pallas_call(body, out_shape=outs, in_specs=specs, out_specs=[VMEM] * l...  11.7 us
    ppermute x4, waiting for transfers between devices, swap(): return lax.ppermute(v, axis, [(0, 1), (1, 0)])  9.17 us
    unnamed x36, local copies, waits for them, and re-layouts  7.92 us
  transfers between devices with their start and end apart: 32, of which 22 were waited for; matrix products, arithmetic and copies ran while one was open for 0% of the time, Pallas kernels for 5%

commit v1 on v0

--- a/solution.py
+++ b/solution.py
@@ -89,7 +89,7 @@
 
     shapes = [((cut, C), BF16), ((rows - cut, C), BF16)]
     fa, fb = call(kernel, shapes, [left, right])
-    return [own, left, right, shift(fa, "x", 1), shift(fb, "x", -1)]
+    return [own, left, right, shift(fa, "x", 1), shift(fb, "x", -1)], fa
 
 
 def x_scatter(right, left, far):
@@ -216,25 +216,43 @@
 
 
 def cot_start_kernel(cot, upw, scale, after, pay):
+    core = lax.axis_index("core")
     pay[0:256, :] = cot[...]
-    pay[256:512, :] = upw[...]
+    pay[256:384, :] = upw[pl.ds(pl.multiple_of(core * 128, 128), 128), :]
     at = lax.broadcasted_iota(jnp.int32, (16, C), 0)
-    rows = after[512:528, :].astype(F32)
+    rows = after[384:400, :].astype(F32)
     for i, row in enumerate(thirds(scale[...])):
         rows = jnp.where(at == i, row, rows)
-    pay[512:528, :] = rows.astype(BF16)
-
-
-def token_kernel(z0, z1, z2, z3, out):
+    pay[384:400, :] = rows.astype(BF16)
+
+
+def halves_kernel(z1, z2, z3, out):
+    for i, z in enumerate((z1, z2, z3)):
+        out[i * 128 : i * 128 + 128, :] = z[256:384, :]
+
+
+def join_halves(zs, other, own, whole):
+    core = lax.axis_index("core")
+    whole[0:256, :] = own[...]
+    for r in (1, 2, 3):
+        mine = pl.ds(pl.multiple_of(r * 256 + core * 128, 128), 128)
+        rest = pl.ds(pl.multiple_of(r * 256 + 128 - core * 128, 128), 128)
+        whole[mine, :] = zs[r][256:384, :]
+        whole[rest, :] = other[r * 128 - 128 : r * 128, :]
+
+
+def token_kernel(z0, z1, z2, z3, other, dn, out, whole):
     a_ref, b_ref = out.at[0:656, :], out.at[656:1296, :]
+    zs = (z0, z1, z2, z3)
+    join_halves(zs, other, dn, whole)
     low = jnp.zeros((T, RANK), F32)
     squares = jnp.zeros((T, 1), F32)
-    for r, z in enumerate((z0, z1, z2, z3)):
+    for r, z in enumerate(zs):
         x = z[:256, :].astype(F32)
-        gain = z[512:528, :].astype(F32)[:1]
+        gain = z[384:400, :].astype(F32)[:1]
         xg = (x * gain).astype(BF16)
         put_blk(a_ref, b_ref, r, 128, xg)
-        low = low + dot(xg, z[256:512, :])
+        low = low + dot(xg, whole[r * 256 : r * 256 + 256, :])
         squares = squares + jnp.sum(x * x, axis=1, keepdims=True)
     low = low.astype(BF16)
     a_ref[512:656, :] = low[:144]
@@ -242,14 +260,18 @@
     b_ref[112:128, :] = tile_of(thirds(line(squares)))
 
 
-def cot_kernel(z0, z1, z2, z3, out):
+def cot_kernel(z0, z1, z2, z3, other, upw, out, whole):
     a_ref, b_ref = out.at[0:640, :], out.at[640:1280, :]
+    zs = (z0, z1, z2, z3)
+    join_halves(zs, other, upw, whole)
     low = jnp.zeros((T, RANK), F32)
-    for r, z in enumerate((z0, z1, z2, z3)):
+    for r, z in enumerate(zs):
         cot = z[:256, :]
-        scale = joined(z[512:528, :].astype(F32), 0)
+        scale = joined(z[384:400, :].astype(F32), 0)
         put_blk(a_ref, b_ref, r, 128, cot)
-        low = low + dot_nt((cot.astype(F32) * scale).astype(BF16), z[256:512, :])
+        low = low + dot_nt(
+            (cot.astype(F32) * scale).astype(BF16), whole[r * 256 : r * 256 + 256, :]
+        )
     low = low.astype(BF16)
     a_ref[512:640, :] = low[:128]
     b_ref[0:128, :] = low[128:]
@@ -477,15 +499,15 @@
 
 
 def out_sum_kernel(
-    own, low_ref, rm, lm, fm, c0, c1, c2, c3, cst, near, far, gos_ref,
+    own, low_ref, rm, lm, fm, c0, c1, c2, c3, whole, cst, near, far, gos_ref,
 ):
     parts = (own, rm, lm, fm)
     low = low_ref[...].astype(F32) + total_of(parts[1:], 1024, 1280)
     lowd = (low * row_of(cst, PICKED + 3)).astype(BF16)
     gos_ref[4:8, :] = jnp.zeros((4, C), F32)
     for r, z in enumerate((c0, c1, c2, c3)):
-        olow = dot(lowd, z[256:512, :])
-        scale = joined(z[512:528, :].astype(F32), 0)
+        olow = dot(lowd, whole[r * 256 : r * 256 + 256, :])
+        scale = joined(z[384:400, :].astype(F32), 0)
         v = total_of(parts, r * 256, r * 256 + 256) + olow * scale
         dst = near if r < 2 else far
         dst[(r % 2) * 256 : (r % 2) * 256 + 256, :] = v.astype(BF16)
@@ -498,7 +520,7 @@
 
 
 def in_sum_kernel(
-    own, rm, lm, fm, z0, z1, z2, z3, gos, o0, o1, o2, o3, keep,
+    own, rm, lm, fm, whole, gos, o0, o1, o2, o3, keep,
 ):
     parts = (own, rm, lm, fm)
     low = total_of(parts, 1024, 1296)
@@ -513,10 +535,9 @@
     common = []
     for row in [inner] + grads:
         common = common + thirds(row)
-    for r, (z, out) in enumerate(((z0, o0), (z1, o1), (z2, o2), (z3, o3))):
-        at = slice(r * 256, r * 256 + 256)
+    for r, out in enumerate((o0, o1, o2, o3)):
         v = total_of(parts, r * 256, r * 256 + 256)
-        v = v + dot_nt(dlow, z[256:512, :])
+        v = v + dot_nt(dlow, whole[r * 256 : r * 256 + 256, :])
         out[0:256, :] = v.astype(out.dtype)
         if r > 0:
             out[256:288, :] = tile_of(common + thirds(gos[r : r + 1, :]), 32)
@@ -616,15 +637,24 @@
         scalars=True,
         hold=[weight, up_in],
     )
-    tz0 = jnp.concatenate([tokens, in_down, gain, jnp.zeros((15, C), BF16)], 0)
+    half = jnp.where(lax.axis_index("core") == 0, in_down[:128], in_down[128:])
+    tz0 = jnp.concatenate([tokens, half, gain, jnp.zeros((15, C), BF16)], 0)
     tz = [tz0] + [across(tz0, "zh", r) for r in (1, 2, 3)]
     (cz0,) = call(
-        cot_start_kernel, [((528, C), BF16)], [cotangent, out_up, out_scale[None], tz[2]]
+        cot_start_kernel, [((400, C), BF16)], [cotangent, out_up, out_scale[None], tz[2]]
     )
     cz = [cz0] + [across(cz0, "zh", r) for r in (1, 2, 3)]
-    (pay,) = call(token_kernel, [((1296, C), BF16)], tz, after=[cst])
-    tr = ring_gather(pay, 656)
-    (cpay,) = call(cot_kernel, [((1280, C), BF16)], cz)
+    (other,) = call(halves_kernel, [((384, C), BF16)], tz[1:], after=[cst])
+    pay, dn_all = call(
+        token_kernel, [((1296, C), BF16), ((1024, C), BF16)],
+        [*tz, swap(other, "core"), in_down],
+    )
+    tr, near_half = ring_gather(pay, 656)
+    (other,) = call(halves_kernel, [((384, C), BF16)], cz[1:], after=[near_half])
+    cpay, up_all = call(
+        cot_kernel, [((1280, C), BF16), ((1024, C), BF16)], [*cz, swap(other, "core"), out_up],
+        after=tr[3:],
+    )
     cr = x_gather(cpay)
     zraw, z, zlow, h, edge, low_raw, rstd = call(
         fwd_in_kernel,
@@ -667,7 +697,7 @@
     got = x_scatter(*out)
     half = [((512, C), BF16)] * 2
     near, far_out, gos = call(
-        out_sum_kernel, half + [((8, C), F32)], [own_out, low_out, *got_out, *cz, cst], after=[sums]
+        out_sum_kernel, half + [((8, C), F32)], [own_out, low_out, *got_out, *cz, up_all, cst], after=[sums]
     )
     keep, send = call(
         out_half_kernel, [((T, C), F32), ((T, C), BF16)], [near, across(far_out, "zh", 2)]
@@ -677,7 +707,7 @@
 
     payload = [((T, C), F32)] + [((288, C), BF16)] * 3 + [((8, C), F32)]
     o0, o1, o2, o3, inner = call(
-        in_sum_kernel, payload, [own, *got, *tz, gos], after=[mixed]
+        in_sum_kernel, payload, [own, *got, dn_all, gos], after=[mixed]
     )
     got = [across(o, "zh", r) for r, o in ((1, o1), (2, o2), (3, o3))]
     grad_tokens, rows = call(

time: 192 us -> 185 us (0.964)
  waiting for transfers between devices: 106 us -> 91.5 us
  starting transfers between devices: 50.5 us -> 54.4 us
  blocking collectives: 12 us -> 14.1 us
    ppermute x15, waiting for transfers between devices: 68.4 us -> 51.1 us  [across(): return lax.ppermute(v, axis, [(i, i ^ bit) for i in range(4)])]
    ppermute x4 -> x6, starting transfers between devices: 3.29 us -> 6.9 us  [swap(): return lax.ppermute(v, axis, [(0, 1), (1, 0)])]
    ppermute x4 -> x6, waiting for transfers between devices: 9.17 us -> 11.3 us  [swap(): return lax.ppermute(v, axis, [(0, 1), (1, 0)])]
    all_to_all x1, blocking collectives: 12 us -> 14.1 us  [ctx_spread(): return lax.all_to_all(wide, CTX, split_axis=0, concat_axis=0, tiled=True)]
    pallas_call x21 -> x23, Pallas kernels: 11.7 us -> 11.9 us  [call(): pl.pallas_call(body, out_shape=outs, in_specs=specs, out_specs=[VMEM] * l...]
    unnamed x36 -> x38, local copies, waits for them, and re-layouts: 7.92 us -> 7.93 us
  transfers between devices with their start and end apart: 32 -> 34, of which waited for: 22 -> 24; matrix products, arithmetic and copies ran while one was open for 0% -> 0% of each run, Pallas kernels for 5% -> 5%
where the time goes in v1:
time: 185 us; the launch traced here: 184 us
  waiting for transfers between devices  91.5 us (49%)
  starting transfers between devices  54.4 us (29%)
  blocking collectives  14.1 us (8%)
  Pallas kernels  11.9 us (6%)
  local copies, waits for them, and re-layouts  8.74 us (5%)
  other arithmetic  2.66 us (1%)
    ppermute x15, waiting for transfers between devices, across(): return lax.ppermute(v, axis, [(i, i ^ bit) for i in range(4)])  51.1 us
    ppermute x15, starting transfers between devices, across(): return lax.ppermute(v, axis, [(i, i ^ bit) for i in range(4)])  32.6 us
    ppermute x13, waiting for transfers between devices, shift(): return lax.ppermute(v, axis, [(i, (i + k) % 4) for i in range(4)])  29.1 us
    ppermute x13, starting transfers between devices, shift(): return lax.ppermute(v, axis, [(i, (i + k) % 4) for i in range(4)])  14.8 us
    all_to_all x1, blocking collectives, ctx_spread(): return lax.all_to_all(wide, CTX, split_axis=0, concat_axis=0, tiled=True)  14.1 us
    pallas_call x23, Pallas kernels, call(): pl.pallas_call(body, out_shape=outs, in_specs=specs, out_specs=[VMEM] * l...  11.9 us
    ppermute x6, waiting for transfers between devices, swap(): return lax.ppermute(v, axis, [(0, 1), (1, 0)])  11.3 us
    unnamed x38, local copies, waits for them, and re-layouts  7.93 us
  transfers between devices with their start and end apart: 34, of which 24 were waited for; matrix products, arithmetic and copies ran while one was open for 0% of the time, Pallas kernels for 5%

profile of v1, /device:TPU:1, one launch (start us, length us, event | category | flops | bytes accessed | tf_op | source)
XLA Modules:
  0.0 184.2 jit_solution(16426586714324353171)
XLA Ops:
  3.4 6.9 %collective-permute-start.2 = (bf16[400,256]{1,0:T(8,128)(2,1)S(1)}, bf16[400,256]{1,0:T(8,128)(2,1)S(1)}, u32[]{:S(2)}, u32[]{:S(2)}) collective-permute-start(bf16[400,256]{1,0:T(8,128)(2,1)S(1)} %maximum_maximum_fusion.z0), channel_id=1, source_target_pairs={{0,3},{1,2},{2,1},{3,0},{4,7},{5,6},{6,5},{7,4},{8,11},{9,10},{10,... | collective-permute-start | bytes 614408 | tf_op jit(solution)/shard_map/ppermute | solution.py:48
  13.2 2.8 %copy-done = bf16[4096,3,256]{2,0,1:T(8,128)(2,1)S(1)} copy-done((bf16[4096,3,256]{2,0,1:T(8,128)(2,1)S(1)}, bf16[4096,3,256]{2,0,1:T(8,128)(2,1)}, u32[]{:S(2)}) %copy-start) | copy-done | bytes 6291480
  21.7 6.2 %collective-permute-done.2.refs_2_.z3 = bf16[400,256]{1,0:T(8,128)(2,1)S(1)} collective-permute-done((bf16[400,256]{1,0:T(8,128)(2,1)S(1)}, bf16[400,256]{1,0:T(8,128)(2,1)S(1)}, u32[]{:S(2)}, u32[]{:S(2)}) %collective-permute-start.2) | collective-permute-done | bytes 204832 | tf_op jit(solution)/shard_map/ppermute | solution.py:48
  27.9 3.8 %collective-permute-done.refs_0_.z1 = bf16[400,256]{1,0:T(8,128)(2,1)S(1)} collective-permute-done((bf16[400,256]{1,0:T(8,128)(2,1)S(1)}, bf16[400,256]{1,0:T(8,128)(2,1)S(1)}, u32[]{:S(2)}, u32[]{:S(2)}) %collective-permute-start) | collective-permute-done | bytes 204832 | tf_op jit(solution)/shard_map/ppermute | solution.py:48
  36.4 2.7 %collective-permute-start.10 = (bf16[400,256]{1,0:T(8,128)(2,1)S(1)}, bf16[400,256]{1,0:T(8,128)(2,1)S(1)}, u32[]{:S(2)}, u32[]{:S(2)}) collective-permute-start(bf16[400,256]{1,0:T(8,128)(2,1)S(1)} %shard_map.204.refs_0_.refs_5_), channel_id=1, source_target_pairs={{0,3},{1,2},{2,1},{3,0},{4,7},{5,6},{6,5},{7,4},{8,11},{9,10},{10,... | collective-permute-start | bytes 614408 | tf_op jit(solution)/shard_map/ppermute | solution.py:48
  42.1 8.1 %collective-permute-done.5.right_ref.refs_2_ = bf16[1296,256]{1,0:T(8,128)(2,1)S(1)} collective-permute-done((bf16[1296,256]{1,0:T(8,128)(2,1)S(1)}, bf16[1296,256]{1,0:T(8,128)(2,1)S(1)}, u32[]{:S(2)}, u32[]{:S(2)}) %collective-permute-start.5) | collective-permute-done | bytes 663584 | tf_op jit(solution)/shard_map/ppermute | solution.py:25
  50.3 3.1 %collective-permute-done.4.left_ref.refs_1_ = bf16[1296,256]{1,0:T(8,128)(2,1)S(1)} collective-permute-done((bf16[1296,256]{1,0:T(8,128)(2,1)S(1)}, bf16[1296,256]{1,0:T(8,128)(2,1)S(1)}, u32[]{:S(2)}, u32[]{:S(2)}) %collective-permute-start.4) | collective-permute-done | bytes 663584 | tf_op jit(solution)/shard_map/ppermute | solution.py:25
  53.5 2.7 %collective-permute-start.7 = (bf16[640,256]{1,0:T(8,128)(2,1)S(1)}, bf16[640,256]{1,0:T(8,128)(2,1)S(1)}, u32[]{:S(2)}, u32[]{:S(2)}) collective-permute-start(bf16[640,256]{1,0:T(8,128)(2,1)S(1)} %get-tuple-element.55), channel_id=1, source_target_pairs={{0,12},{4,0},{8,4},{12,8},{1,13},{5,1},{9,5},{13,9},{2,14},{6,2},{... | collective-permute-start | bytes 983048 | tf_op jit(solution)/shard_map/ppermute | solution.py:25
  56.2 5.2 %collective-permute-done.8.refs_0_.refs_1_.refs_6_ = bf16[400,256]{1,0:T(8,128)(2,1)S(1)} collective-permute-done((bf16[400,256]{1,0:T(8,128)(2,1)S(1)}, bf16[400,256]{1,0:T(8,128)(2,1)S(1)}, u32[]{:S(2)}, u32[]{:S(2)}) %collective-permute-start.8) | collective-permute-done | bytes 204832 | tf_op jit(solution)/shard_map/ppermute | solution.py:48
  75.5 2.9 %collective-permute-start.14 = (f32[2,2,16,256]{3,2,1,0:T(8,128)S(1)}, f32[2,2,16,256]{3,2,1,0:T(8,128)S(1)}, u32[]{:S(2)}, u32[]{:S(2)}) collective-permute-start(f32[2,2,16,256]{3,2,1,0:T(8,128)S(1)} %shard_map.209.refs_0_), channel_id=1, source_target_pairs={{0,64},{32,96},{64,0},{96,32},{1,65},{33,97},{65,1},{97,33},{2,66}... | collective-permute-start | bytes 196616 | tf_op jit(solution)/shard_map/ppermute | solution.py:48
  80.5 4.1 %collective-permute-done.15.other = f32[2,2,2,16,256]{4,3,2,1,0:T(8,128)S(1)} collective-permute-done((f32[2,2,2,16,256]{4,3,2,1,0:T(8,128)S(1)}, f32[2,2,2,16,256]{4,3,2,1,0:T(8,128)S(1)}, u32[]{:S(2)}, u32[]{:S(2)}) %collective-permute-start.15) | collective-permute-done | bytes 131104 | tf_op jit(solution)/shard_map/ppermute | solution.py:29
  89.5 5.0 %collective-permute-done.20.refs_2_ = bf16[1280,256]{1,0:T(8,128)(2,1)S(1)} collective-permute-done((bf16[1280,256]{1,0:T(8,128)(2,1)S(1)}, bf16[1280,256]{1,0:T(8,128)(2,1)S(1)}, u32[]{:S(2)}, u32[]{:S(2)}) %collective-permute-start.20) | collective-permute-done | bytes 655392 | tf_op jit(solution)/shard_map/ppermute | solution.py:25
  96.8 3.2 %collective-permute-start.22 = (f32[8,256]{1,0:T(8,128)S(1)}, f32[8,256]{1,0:T(8,128)S(1)}, u32[]{:S(2)}, u32[]{:S(2)}) collective-permute-start(f32[8,256]{1,0:T(8,128)S(1)} %get-tuple-element.68.refs_0_), channel_id=1, source_target_pairs={{0,16},{16,0},{1,17},{17,1},{2,18},{18,2},{3,19},{19,3},{4,20},{20... | collective-permute-start | bytes 24584 | tf_op jit(solution)/shard_map/ppermute | solution.py:29
  103.7 2.9 %collective-permute-start.24 = (f32[2,2,8,256]{3,2,1,0:T(8,128)S(1)}, f32[2,2,8,256]{3,2,1,0:T(8,128)S(1)}, u32[]{:S(2)}, u32[]{:S(2)}) collective-permute-start(f32[2,2,8,256]{3,2,1,0:T(8,128)S(1)} %shard_map.215.refs_0_), channel_id=1, source_target_pairs={{0,64},{32,96},{64,0},{96,32},{1,65},{33,97},{65,1},{97,33},{2,66}... | collective-permute-start | bytes 98312 | tf_op jit(solution)/shard_map/ppermute | solution.py:48
  108.0 3.4 %collective-permute-done.25.other = f32[2,2,2,8,256]{4,3,2,1,0:T(8,128)S(1)} collective-permute-done((f32[2,2,2,8,256]{4,3,2,1,0:T(8,128)S(1)}, f32[2,2,2,8,256]{4,3,2,1,0:T(8,128)S(1)}, u32[]{:S(2)}, u32[]{:S(2)}) %collective-permute-start.25) | collective-permute-done | bytes 65568 | tf_op jit(solution)/shard_map/ppermute | solution.py:29
  113.9 2.7 %collective-permute-start.29 = (bf16[1296,256]{1,0:T(8,128)(2,1)S(1)}, bf16[1296,256]{1,0:T(8,128)(2,1)S(1)}, u32[]{:S(2)}, u32[]{:S(2)}) collective-permute-start(bf16[1296,256]{1,0:T(8,128)(2,1)S(1)} %get-tuple-element.87), channel_id=1, source_target_pairs={{0,12},{4,0},{8,4},{12,8},{1,13},{5,1},{9,5},{13,9},{2,14},{6,2},{... | collective-permute-start | bytes 1990664 | tf_op jit(solution)/shard_map/ppermute | solution.py:25
  116.6 4.9 %collective-permute-done.18.refs_4_ = bf16[1280,256]{1,0:T(8,128)(2,1)S(1)} collective-permute-done((bf16[1280,256]{1,0:T(8,128)(2,1)S(1)}, bf16[1280,256]{1,0:T(8,128)(2,1)S(1)}, u32[]{:S(2)}, u32[]{:S(2)}) %collective-permute-start.18) | collective-permute-done | bytes 655392 | tf_op jit(solution)/shard_map/ppermute | solution.py:25
  122.1 3.5 %collective-permute-start.26 = (bf16[512,256]{1,0:T(8,128)(2,1)S(1)}, bf16[512,256]{1,0:T(8,128)(2,1)S(1)}, u32[]{:S(2)}, u32[]{:S(2)}) collective-permute-start(bf16[512,256]{1,0:T(8,128)(2,1)S(1)} %get-tuple-element.82), channel_id=1, source_target_pairs={{0,2},{1,3},{2,0},{3,1},{4,6},{5,7},{6,4},{7,5},{8,10},{9,11},{10,... | collective-permute-start | bytes 786440 | tf_op jit(solution)/shard_map/ppermute | solution.py:48
  125.6 8.7 %collective-permute-done.26.far = bf16[512,256]{1,0:T(8,128)(2,1)S(1)} collective-permute-done((bf16[512,256]{1,0:T(8,128)(2,1)S(1)}, bf16[512,256]{1,0:T(8,128)(2,1)S(1)}, u32[]{:S(2)}, u32[]{:S(2)}) %collective-permute-start.26) | collective-permute-done | bytes 262176 | tf_op jit(solution)/shard_map/ppermute | solution.py:48
  134.4 8.7 %collective-permute-done.27 = bf16[256,256]{1,0:T(8,128)(2,1)S(1)} collective-permute-done((bf16[256,256]{1,0:T(8,128)(2,1)S(1)}, bf16[256,256]{1,0:T(8,128)(2,1)S(1)}, u32[]{:S(2)}, u32[]{:S(2)}) %collective-permute-start.27) | collective-permute-done | bytes 131104 | tf_op jit(solution)/shard_map/ppermute | solution.py:48
  143.2 6.8 %collective-permute-done.30.refs_3_ = bf16[1296,256]{1,0:T(8,128)(2,1)S(1)} collective-permute-done((bf16[1296,256]{1,0:T(8,128)(2,1)S(1)}, bf16[1296,256]{1,0:T(8,128)(2,1)S(1)}, u32[]{:S(2)}, u32[]{:S(2)}) %collective-permute-start.30) | collective-permute-done | bytes 663584 | tf_op jit(solution)/shard_map/ppermute | solution.py:25
  150.6 3.6 %collective-permute-start.32 = (bf16[288,256]{1,0:T(8,128)(2,1)S(1)}, bf16[288,256]{1,0:T(8,128)(2,1)S(1)}, u32[]{:S(2)}, u32[]{:S(2)}) collective-permute-start(bf16[288,256]{1,0:T(8,128)(2,1)S(1)} %get-tuple-element.93), channel_id=1, source_target_pairs={{0,2},{1,3},{2,0},{3,1},{4,6},{5,7},{6,4},{7,5},{8,10},{9,11},{10,... | collective-permute-start | bytes 442376 | tf_op jit(solution)/shard_map/ppermute | solution.py:48
  158.6 9.3 %collective-permute-done.33.r3 = bf16[288,256]{1,0:T(8,128)(2,1)S(1)} collective-permute-done((bf16[288,256]{1,0:T(8,128)(2,1)S(1)}, bf16[288,256]{1,0:T(8,128)(2,1)S(1)}, u32[]{:S(2)}, u32[]{:S(2)}) %collective-permute-start.33) | collective-permute-done | bytes 147488 | tf_op jit(solution)/shard_map/ppermute | solution.py:48
  168.9 14.1 %all_to_all.5.rep = f32[16,8,256]{2,1,0:T(8,128)S(1)} all-to-all(f32[16,8,256]{2,1,0:T(8,128)S(1)} %broadcast_in_dim.30), channel_id=1, replica_groups=mesh['zl'=2,'y'=4,'core'=2,'x'=4,'zh'=4] {'zl','y','core'}, dimensions={0} | all-to-all | bytes 262144 | tf_op jit(solution)/shard_map/all_to_all | solution.py:53
  (114 shorter events, 58.0 us)
Async XLA Ops:
  3.4 24.5 %collective-permute-start.2 = (bf16[400,256]{1,0:T(8,128)(2,1)S(1)}, bf16[400,256]{1,0:T(8,128)(2,1)S(1)}, u32[]{:S(2)}, u32[]{:S(2)}) collective-permute-start(bf16[400,256]{1,0:T(8,128)(2,1)S(1)} %maximum_maximum_fusion.z0), channel_id=1, source_target_pairs={{0,3},{1,2},{2,1},{3,0},{4,7},{5,6},{6,5},{7,4},{8,11},{9,10},{10,... | collective-permute-start | bytes 614408 | tf_op jit(solution)/shard_map/ppermute | solution.py:48
  10.3 17.5 %collective-permute-start.1 = (bf16[400,256]{1,0:T(8,128)(2,1)S(1)}, bf16[400,256]{1,0:T(8,128)(2,1)S(1)}, u32[]{:S(2)}, u32[]{:S(2)}) collective-permute-start(bf16[400,256]{1,0:T(8,128)(2,1)S(1)} %maximum_maximum_fusion.z0), channel_id=1, source_target_pairs={{0,2},{1,3},{2,0},{3,1},{4,6},{5,7},{6,4},{7,5},{8,10},{9,11},{10,... | collective-permute-start | bytes 614408 | tf_op jit(solution)/shard_map/ppermute | solution.py:48
  11.3 20.4 %collective-permute-start = (bf16[400,256]{1,0:T(8,128)(2,1)S(1)}, bf16[400,256]{1,0:T(8,128)(2,1)S(1)}, u32[]{:S(2)}, u32[]{:S(2)}) collective-permute-start(bf16[400,256]{1,0:T(8,128)(2,1)S(1)} %maximum_maximum_fusion.z0), channel_id=1, source_target_pairs={{0,1},{1,0},{2,3},{3,2},{4,5},{5,4},{6,7},{7,6},{8,9},{9,8},{10,11... | collective-permute-start | bytes 614408 | tf_op jit(solution)/shard_map/ppermute | solution.py:48
  33.8 16.5 %collective-permute-start.5 = (bf16[1296,256]{1,0:T(8,128)(2,1)S(1)}, bf16[1296,256]{1,0:T(8,128)(2,1)S(1)}, u32[]{:S(2)}, u32[]{:S(2)}) collective-permute-start(bf16[1296,256]{1,0:T(8,128)(2,1)S(1)} %get-tuple-element.53.refs_0_), channel_id=1, source_target_pairs={{0,12},{4,0},{8,4},{12,8},{1,13},{5,1},{9,5},{13,9},{2,14},{6,2},{... | collective-permute-start | bytes 1990664 | tf_op jit(solution)/shard_map/ppermute | solution.py:25
  36.4 17.0 %collective-permute-start.4 = (bf16[1296,256]{1,0:T(8,128)(2,1)S(1)}, bf16[1296,256]{1,0:T(8,128)(2,1)S(1)}, u32[]{:S(2)}, u32[]{:S(2)}) collective-permute-start(bf16[1296,256]{1,0:T(8,128)(2,1)S(1)} %get-tuple-element.53.refs_0_), channel_id=1, source_target_pairs={{0,4},{4,8},{8,12},{12,0},{1,5},{5,9},{9,13},{13,1},{2,6},{6,10},{... | collective-permute-start | bytes 1990664 | tf_op jit(solution)/shard_map/ppermute | solution.py:25
  36.4 19.8 %collective-permute-start.10 = (bf16[400,256]{1,0:T(8,128)(2,1)S(1)}, bf16[400,256]{1,0:T(8,128)(2,1)S(1)}, u32[]{:S(2)}, u32[]{:S(2)}) collective-permute-start(bf16[400,256]{1,0:T(8,128)(2,1)S(1)} %shard_map.204.refs_0_.refs_5_), channel_id=1, source_target_pairs={{0,3},{1,2},{2,1},{3,0},{4,7},{5,6},{6,5},{7,4},{8,11},{9,10},{10,... | collective-permute-start | bytes 614408 | tf_op jit(solution)/shard_map/ppermute | solution.py:48
  39.1 17.1 %collective-permute-start.9 = (bf16[400,256]{1,0:T(8,128)(2,1)S(1)}, bf16[400,256]{1,0:T(8,128)(2,1)S(1)}, u32[]{:S(2)}, u32[]{:S(2)}) collective-permute-start(bf16[400,256]{1,0:T(8,128)(2,1)S(1)} %shard_map.204.refs_0_.refs_5_), channel_id=1, source_target_pairs={{0,2},{1,3},{2,0},{3,1},{4,6},{5,7},{6,4},{7,5},{8,10},{9,11},{10,... | collective-permute-start | bytes 614408 | tf_op jit(solution)/shard_map/ppermute | solution.py:48
  41.0 20.4 %collective-permute-start.8 = (bf16[400,256]{1,0:T(8,128)(2,1)S(1)}, bf16[400,256]{1,0:T(8,128)(2,1)S(1)}, u32[]{:S(2)}, u32[]{:S(2)}) collective-permute-start(bf16[400,256]{1,0:T(8,128)(2,1)S(1)} %shard_map.204.refs_0_.refs_5_), channel_id=1, source_target_pairs={{0,1},{1,0},{2,3},{3,2},{4,5},{5,4},{6,7},{7,6},{8,9},{9,8},{10,11... | collective-permute-start | bytes 614408 | tf_op jit(solution)/shard_map/ppermute | solution.py:48
  53.4 9.6 %collective-permute-start.6 = (bf16[656,256]{1,0:T(8,128)(2,1)S(1)}, bf16[656,256]{1,0:T(8,128)(2,1)S(1)}, u32[]{:S(2)}, u32[]{:S(2)}) collective-permute-start(bf16[656,256]{1,0:T(8,128)(2,1)S(1)} %get-tuple-element.54.refs_3_), channel_id=1, source_target_pairs={{0,4},{4,8},{8,12},{12,0},{1,5},{5,9},{9,13},{13,1},{2,6},{6,10},{... | collective-permute-start | bytes 1007624 | tf_op jit(solution)/shard_map/ppermute | solution.py:25
  53.5 9.5 %collective-permute-start.7 = (bf16[640,256]{1,0:T(8,128)(2,1)S(1)}, bf16[640,256]{1,0:T(8,128)(2,1)S(1)}, u32[]{:S(2)}, u32[]{:S(2)}) collective-permute-start(bf16[640,256]{1,0:T(8,128)(2,1)S(1)} %get-tuple-element.55), channel_id=1, source_target_pairs={{0,12},{4,0},{8,4},{12,8},{1,13},{5,1},{9,5},{13,9},{2,14},{6,2},{... | collective-permute-start | bytes 983048 | tf_op jit(solution)/shard_map/ppermute | solution.py:25
  63.4 25.4 %collective-permute-start.21 = (bf16[1280,256]{1,0:T(8,128)(2,1)S(1)}, bf16[1280,256]{1,0:T(8,128)(2,1)S(1)}, u32[]{:S(2)}, u32[]{:S(2)}) collective-permute-start(bf16[1280,256]{1,0:T(8,128)(2,1)S(1)} %get-tuple-element.56.refs_8_.refs_0_), channel_id=1, source_target_pairs={{0,8},{4,12},{8,0},{12,4},{1,9},{5,13},{9,1},{13,5},{2,10},{6,14},... | collective-permute-start | bytes 1966088 | tf_op jit(solution)/shard_map/ppermute | solution.py:25
  65.2 29.3 %collective-permute-start.20 = (bf16[1280,256]{1,0:T(8,128)(2,1)S(1)}, bf16[1280,256]{1,0:T(8,128)(2,1)S(1)}, u32[]{:S(2)}, u32[]{:S(2)}) collective-permute-start(bf16[1280,256]{1,0:T(8,128)(2,1)S(1)} %get-tuple-element.56.refs_8_.refs_0_), channel_id=1, source_target_pairs={{0,12},{4,0},{8,4},{12,8},{1,13},{5,1},{9,5},{13,9},{2,14},{6,2},{... | collective-permute-start | bytes 1966088 | tf_op jit(solution)/shard_map/ppermute | solution.py:25
  66.3 29.4 %collective-permute-start.19 = (bf16[1280,256]{1,0:T(8,128)(2,1)S(1)}, bf16[1280,256]{1,0:T(8,128)(2,1)S(1)}, u32[]{:S(2)}, u32[]{:S(2)}) collective-permute-start(bf16[1280,256]{1,0:T(8,128)(2,1)S(1)} %get-tuple-element.56.refs_8_.refs_0_), channel_id=1, source_target_pairs={{0,4},{4,8},{8,12},{12,0},{1,5},{5,9},{9,13},{13,1},{2,6},{6,10},{... | collective-permute-start | bytes 1966088 | tf_op jit(solution)/shard_map/ppermute | solution.py:25
  86.1 30.5 %collective-permute-start.16 = (bf16[1280,256]{1,0:T(8,128)(2,1)S(1)}, bf16[1280,256]{1,0:T(8,128)(2,1)S(1)}, u32[]{:S(2)}, u32[]{:S(2)}) collective-permute-start(bf16[1280,256]{1,0:T(8,128)(2,1)S(1)} %get-tuple-element.63), channel_id=1, source_target_pairs={{0,4},{4,8},{8,12},{12,0},{1,5},{5,9},{9,13},{13,1},{2,6},{6,10},{... | collective-permute-start | bytes 1966088 | tf_op jit(solution)/shard_map/ppermute | solution.py:25
  87.6 28.9 %collective-permute-start.17 = (bf16[1280,256]{1,0:T(8,128)(2,1)S(1)}, bf16[1280,256]{1,0:T(8,128)(2,1)S(1)}, u32[]{:S(2)}, u32[]{:S(2)}) collective-permute-start(bf16[1280,256]{1,0:T(8,128)(2,1)S(1)} %get-tuple-element.64), channel_id=1, source_target_pairs={{0,12},{4,0},{8,4},{12,8},{1,13},{5,1},{9,5},{13,9},{2,14},{6,2},{... | collective-permute-start | bytes 1966088 | tf_op jit(solution)/shard_map/ppermute | solution.py:25
  88.8 32.7 %collective-permute-start.18 = (bf16[1280,256]{1,0:T(8,128)(2,1)S(1)}, bf16[1280,256]{1,0:T(8,128)(2,1)S(1)}, u32[]{:S(2)}, u32[]{:S(2)}) collective-permute-start(bf16[1280,256]{1,0:T(8,128)(2,1)S(1)} %get-tuple-element.65), channel_id=1, source_target_pairs={{0,8},{4,12},{8,0},{12,4},{1,9},{5,13},{9,1},{13,5},{2,10},{6,14},... | collective-permute-start | bytes 1966088 | tf_op jit(solution)/shard_map/ppermute | solution.py:25
  113.8 29.3 %collective-permute-start.28 = (bf16[1296,256]{1,0:T(8,128)(2,1)S(1)}, bf16[1296,256]{1,0:T(8,128)(2,1)S(1)}, u32[]{:S(2)}, u32[]{:S(2)}) collective-permute-start(bf16[1296,256]{1,0:T(8,128)(2,1)S(1)} %get-tuple-element.86), channel_id=1, source_target_pairs={{0,4},{4,8},{8,12},{12,0},{1,5},{5,9},{9,13},{13,1},{2,6},{6,10},{... | collective-permute-start | bytes 1990664 | tf_op jit(solution)/shard_map/ppermute | solution.py:25
  113.9 29.3 %collective-permute-start.29 = (bf16[1296,256]{1,0:T(8,128)(2,1)S(1)}, bf16[1296,256]{1,0:T(8,128)(2,1)S(1)}, u32[]{:S(2)}, u32[]{:S(2)}) collective-permute-start(bf16[1296,256]{1,0:T(8,128)(2,1)S(1)} %get-tuple-element.87), channel_id=1, source_target_pairs={{0,12},{4,0},{8,4},{12,8},{1,13},{5,1},{9,5},{13,9},{2,14},{6,2},{... | collective-permute-start | bytes 1990664 | tf_op jit(solution)/shard_map/ppermute | solution.py:25
  116.6 33.4 %collective-permute-start.30 = (bf16[1296,256]{1,0:T(8,128)(2,1)S(1)}, bf16[1296,256]{1,0:T(8,128)(2,1)S(1)}, u32[]{:S(2)}, u32[]{:S(2)}) collective-permute-start(bf16[1296,256]{1,0:T(8,128)(2,1)S(1)} %get-tuple-element.88), channel_id=1, source_target_pairs={{0,8},{4,12},{8,0},{12,4},{1,9},{5,13},{9,1},{13,5},{2,10},{6,14},... | collective-permute-start | bytes 1990664 | tf_op jit(solution)/shard_map/ppermute | solution.py:25
  122.1 12.2 %collective-permute-start.26 = (bf16[512,256]{1,0:T(8,128)(2,1)S(1)}, bf16[512,256]{1,0:T(8,128)(2,1)S(1)}, u32[]{:S(2)}, u32[]{:S(2)}) collective-permute-start(bf16[512,256]{1,0:T(8,128)(2,1)S(1)} %get-tuple-element.82), channel_id=1, source_target_pairs={{0,2},{1,3},{2,0},{3,1},{4,6},{5,7},{6,4},{7,5},{8,10},{9,11},{10,... | collective-permute-start | bytes 786440 | tf_op jit(solution)/shard_map/ppermute | solution.py:48
  134.3 8.8 %collective-permute-start.27 = (bf16[256,256]{1,0:T(8,128)(2,1)S(1)}, bf16[256,256]{1,0:T(8,128)(2,1)S(1)}, u32[]{:S(2)}, u32[]{:S(2)}) collective-permute-start(bf16[256,256]{1,0:T(8,128)(2,1)S(1)} %get-tuple-element.84), channel_id=1, source_target_pairs={{0,1},{1,0},{2,3},{3,2},{4,5},{5,4},{6,7},{7,6},{8,9},{9,8},{10,11... | collective-permute-start | bytes 393224 | tf_op jit(solution)/shard_map/ppermute | solution.py:48
  150.4 6.3 %collective-permute-start.31 = (bf16[288,256]{1,0:T(8,128)(2,1)S(1)}, bf16[288,256]{1,0:T(8,128)(2,1)S(1)}, u32[]{:S(2)}, u32[]{:S(2)}) collective-permute-start(bf16[288,256]{1,0:T(8,128)(2,1)S(1)} %get-tuple-element.92), channel_id=1, source_target_pairs={{0,1},{1,0},{2,3},{3,2},{4,5},{5,4},{6,7},{7,6},{8,9},{9,8},{10,11... | collective-permute-start | bytes 442376 | tf_op jit(solution)/shard_map/ppermute | solution.py:48
  150.6 8.0 %collective-permute-start.32 = (bf16[288,256]{1,0:T(8,128)(2,1)S(1)}, bf16[288,256]{1,0:T(8,128)(2,1)S(1)}, u32[]{:S(2)}, u32[]{:S(2)}) collective-permute-start(bf16[288,256]{1,0:T(8,128)(2,1)S(1)} %get-tuple-element.93), channel_id=1, source_target_pairs={{0,2},{1,3},{2,0},{3,1},{4,6},{5,7},{6,4},{7,5},{8,10},{9,11},{10,... | collective-permute-start | bytes 442376 | tf_op jit(solution)/shard_map/ppermute | solution.py:48
  154.2 13.8 %collective-permute-start.33 = (bf16[288,256]{1,0:T(8,128)(2,1)S(1)}, bf16[288,256]{1,0:T(8,128)(2,1)S(1)}, u32[]{:S(2)}, u32[]{:S(2)}) collective-permute-start(bf16[288,256]{1,0:T(8,128)(2,1)S(1)} %get-tuple-element.94), channel_id=1, source_target_pairs={{0,3},{1,2},{2,1},{3,0},{4,7},{5,6},{6,5},{7,4},{8,11},{9,10},{10,... | collective-permute-start | bytes 442376 | tf_op jit(solution)/shard_map/ppermute | solution.py:48
  (29 other events, 461.6 us)

commit v2 on v1

--- a/solution.py
+++ b/solution.py
@@ -383,15 +383,24 @@
         next_ref[3 + 2 * i : 4 + 2 * i, :] = following(first1[i])
 
 
-def part_kernel(gated_ref, low_ref, ow_ref, right_ref, left_ref, far_ref, own_ref):
+def part_kernel(gated_ref, low_ref, ow_ref, right_ref, left_ref, own_ref):
     ids = block_ids()
     gated = gated_ref[...]
-    for k, dst in ((3, far_ref), (2, right_ref), (1, left_ref), (0, own_ref)):
+    for k, dst in ((2, right_ref), (1, left_ref), (0, own_ref)):
         if k > 0:
             dst[1024:1280, :] = low_ref[...]
         for r in range(4):
             cols = pl.ds(pl.multiple_of(ids[k][r] * 256, 256), 256)
             dst[r * 256 : r * 256 + 256, :] = dot(gated, ow_ref[:, cols]).astype(BF16)
+
+
+def far_part_kernel(gated_ref, low_ref, ow_ref, far_ref):
+    ids = block_ids()
+    gated = gated_ref[...]
+    far_ref[1024:1280, :] = low_ref[...]
+    for r in range(4):
+        cols = pl.ds(pl.multiple_of(ids[3][r] * 256, 256), 256)
+        far_ref[r * 256 : r * 256 + 256, :] = dot(gated, ow_ref[:, cols]).astype(BF16)
 
 
 def bwd_in_kernel(
@@ -671,13 +680,12 @@
         [*edges, z, h, cst, out_down],
         scratch=[pltpu.VMEM((SLABS, 16, C), F32)],
     )
-    *out, own_out = call(
+    to_right, to_left, own_out = call(
         part_kernel,
-        [((1280, C), BF16)] * 3 + [((1024, C), BF16)],
+        [((1280, C), BF16)] * 2 + [((1024, C), BF16)],
         [gated, low_out, out_weight],
         flops=2 * T * WIDTH * C,
     )
-    got_out = x_scatter(*out)
     dg, gsum, gedge, last = call(
         bwd_in_kernel,
         [((T, C), F32), ((T, C), F32), ((8, C), F32), ((8, RANK), F32)],
@@ -685,6 +693,10 @@
         after=[own_out],
         flops=2 * T * WIDTH * C,
     )
+    (to_far,) = call(
+        far_part_kernel, [((1280, C), BF16)], [gated, low_out, out_weight], after=[dg]
+    )
+    got_out = x_scatter(to_right, to_left, to_far)
     gedges, _ = ctx_gather(gedge)
     *out, own, sums = call(
         bwd_out_kernel,

time: 185 us -> 184 us (level)
    ppermute x13, starting transfers between devices: 14.8 us -> 17.3 us  [shift(): return lax.ppermute(v, axis, [(i, (i + k) % 4) for i in range(4)])]
    pallas_call x23 -> x24, Pallas kernels: 11.9 us -> 12.1 us  [call(): pl.pallas_call(body, out_shape=outs, in_specs=specs, out_specs=[VMEM] * l...]
where the time goes in v2:
time: 184 us
  waiting for transfers between devices  90 us (49%)
  starting transfers between devices  55.7 us (30%)
  blocking collectives  14 us (8%)
  Pallas kernels  12.1 us (7%)
  local copies, waits for them, and re-layouts  8.74 us (5%)
  other arithmetic  2.66 us (1%)
    ppermute x15, waiting for transfers between devices, across(): return lax.ppermute(v, axis, [(i, i ^ bit) for i in range(4)])  51.1 us
    ppermute x15, starting transfers between devices, across(): return lax.ppermute(v, axis, [(i, i ^ bit) for i in range(4)])  32.6 us
    ppermute x13, waiting for transfers between devices, shift(): return lax.ppermute(v, axis, [(i, (i + k) % 4) for i in range(4)])  27.6 us
    ppermute x13, starting transfers between devices, shift(): return lax.ppermute(v, axis, [(i, (i + k) % 4) for i in range(4)])  17.3 us
    all_to_all x1, blocking collectives, ctx_spread(): return lax.all_to_all(wide, CTX, split_axis=0, concat_axis=0, tiled=True)  14 us
    pallas_call x24, Pallas kernels, call(): pl.pallas_call(body, out_shape=outs, in_specs=specs, out_specs=[VMEM] * l...  12.1 us
    ppermute x6, waiting for transfers between devices, swap(): return lax.ppermute(v, axis, [(0, 1), (1, 0)])  11.3 us
    unnamed x38, local copies, waits for them, and re-layouts  7.93 us
  transfers between devices with their start and end apart: 34, of which 24 were waited for; matrix products, arithmetic and copies ran while one was open for 0% of the time, Pallas kernels for 5%

profile of v2, /device:TPU:1, one launch (start us, length us, event | category | flops | bytes accessed | tf_op | source)
XLA Modules:
  0.0 184.1 jit_solution(2424204151964863769)
XLA Ops:
  3.4 6.9 %collective-permute-start.2 = (bf16[400,256]{1,0:T(8,128)(2,1)S(1)}, bf16[400,256]{1,0:T(8,128)(2,1)S(1)}, u32[]{:S(2)}, u32[]{:S(2)}) collective-permute-start(bf16[400,256]{1,0:T(8,128)(2,1)S(1)} %maximum_maximum_fusion.z0), channel_id=1, source_target_pairs={{0,3},{1,2},{2,1},{3,0},{4,7},{5,6},{6,5},{7,4},{8,11},{9,10},{10,... | collective-permute-start | bytes 614408 | tf_op jit(solution)/shard_map/ppermute | solution.py:48
  13.2 2.8 %copy-done = bf16[4096,3,256]{2,0,1:T(8,128)(2,1)S(1)} copy-done((bf16[4096,3,256]{2,0,1:T(8,128)(2,1)S(1)}, bf16[4096,3,256]{2,0,1:T(8,128)(2,1)}, u32[]{:S(2)}) %copy-start) | copy-done | bytes 6291480
  21.7 6.2 %collective-permute-done.2.refs_2_.z3 = bf16[400,256]{1,0:T(8,128)(2,1)S(1)} collective-permute-done((bf16[400,256]{1,0:T(8,128)(2,1)S(1)}, bf16[400,256]{1,0:T(8,128)(2,1)S(1)}, u32[]{:S(2)}, u32[]{:S(2)}) %collective-permute-start.2) | collective-permute-done | bytes 204832 | tf_op jit(solution)/shard_map/ppermute | solution.py:48
  27.9 3.8 %collective-permute-done.refs_0_.z1 = bf16[400,256]{1,0:T(8,128)(2,1)S(1)} collective-permute-done((bf16[400,256]{1,0:T(8,128)(2,1)S(1)}, bf16[400,256]{1,0:T(8,128)(2,1)S(1)}, u32[]{:S(2)}, u32[]{:S(2)}) %collective-permute-start) | collective-permute-done | bytes 204832 | tf_op jit(solution)/shard_map/ppermute | solution.py:48
  33.8 2.6 %collective-permute-start.5 = (bf16[1296,256]{1,0:T(8,128)(2,1)S(1)}, bf16[1296,256]{1,0:T(8,128)(2,1)S(1)}, u32[]{:S(2)}, u32[]{:S(2)}) collective-permute-start(bf16[1296,256]{1,0:T(8,128)(2,1)S(1)} %get-tuple-element.52.refs_0_), channel_id=1, source_target_pairs={{0,12},{4,0},{8,4},{12,8},{1,13},{5,1},{9,5},{13,9},{2,14},{6,2},{... | collective-permute-start | bytes 1990664 | tf_op jit(solution)/shard_map/ppermute | solution.py:25
  36.4 2.7 %collective-permute-start.10 = (bf16[400,256]{1,0:T(8,128)(2,1)S(1)}, bf16[400,256]{1,0:T(8,128)(2,1)S(1)}, u32[]{:S(2)}, u32[]{:S(2)}) collective-permute-start(bf16[400,256]{1,0:T(8,128)(2,1)S(1)} %shard_map.204.refs_0_.refs_5_), channel_id=1, source_target_pairs={{0,3},{1,2},{2,1},{3,0},{4,7},{5,6},{6,5},{7,4},{8,11},{9,10},{10,... | collective-permute-start | bytes 614408 | tf_op jit(solution)/shard_map/ppermute | solution.py:48
  42.1 8.1 %collective-permute-done.5.right_ref.refs_2_ = bf16[1296,256]{1,0:T(8,128)(2,1)S(1)} collective-permute-done((bf16[1296,256]{1,0:T(8,128)(2,1)S(1)}, bf16[1296,256]{1,0:T(8,128)(2,1)S(1)}, u32[]{:S(2)}, u32[]{:S(2)}) %collective-permute-start.5) | collective-permute-done | bytes 663584 | tf_op jit(solution)/shard_map/ppermute | solution.py:25
  50.3 3.1 %collective-permute-done.4.left_ref.refs_1_ = bf16[1296,256]{1,0:T(8,128)(2,1)S(1)} collective-permute-done((bf16[1296,256]{1,0:T(8,128)(2,1)S(1)}, bf16[1296,256]{1,0:T(8,128)(2,1)S(1)}, u32[]{:S(2)}, u32[]{:S(2)}) %collective-permute-start.4) | collective-permute-done | bytes 663584 | tf_op jit(solution)/shard_map/ppermute | solution.py:25
  53.5 2.7 %collective-permute-start.7 = (bf16[640,256]{1,0:T(8,128)(2,1)S(1)}, bf16[640,256]{1,0:T(8,128)(2,1)S(1)}, u32[]{:S(2)}, u32[]{:S(2)}) collective-permute-start(bf16[640,256]{1,0:T(8,128)(2,1)S(1)} %get-tuple-element.54), channel_id=1, source_target_pairs={{0,12},{4,0},{8,4},{12,8},{1,13},{5,1},{9,5},{13,9},{2,14},{6,2},{... | collective-permute-start | bytes 983048 | tf_op jit(solution)/shard_map/ppermute | solution.py:25
  56.2 5.2 %collective-permute-done.8.refs_0_.refs_1_.refs_6_ = bf16[400,256]{1,0:T(8,128)(2,1)S(1)} collective-permute-done((bf16[400,256]{1,0:T(8,128)(2,1)S(1)}, bf16[400,256]{1,0:T(8,128)(2,1)S(1)}, u32[]{:S(2)}, u32[]{:S(2)}) %collective-permute-start.8) | collective-permute-done | bytes 204832 | tf_op jit(solution)/shard_map/ppermute | solution.py:48
  69.1 2.5 %collective-permute-start.12 = (f32[16,256]{1,0:T(8,128)S(1)}, f32[16,256]{1,0:T(8,128)S(1)}, u32[]{:S(2)}, u32[]{:S(2)}) collective-permute-start(f32[16,256]{1,0:T(8,128)S(1)} %get-tuple-element.56.refs_0_), channel_id=1, source_target_pairs={{0,16},{16,0},{1,17},{17,1},{2,18},{18,2},{3,19},{19,3},{4,20},{20... | collective-permute-start | bytes 49160 | tf_op jit(solution)/shard_map/ppermute | solution.py:29
  75.5 2.9 %collective-permute-start.14 = (f32[2,2,16,256]{3,2,1,0:T(8,128)S(1)}, f32[2,2,16,256]{3,2,1,0:T(8,128)S(1)}, u32[]{:S(2)}, u32[]{:S(2)}) collective-permute-start(f32[2,2,16,256]{3,2,1,0:T(8,128)S(1)} %shard_map.209.refs_0_), channel_id=1, source_target_pairs={{0,64},{32,96},{64,0},{96,32},{1,65},{33,97},{65,1},{97,33},{2,66}... | collective-permute-start | bytes 196616 | tf_op jit(solution)/shard_map/ppermute | solution.py:48
  80.5 4.1 %collective-permute-done.15.other = f32[2,2,2,16,256]{4,3,2,1,0:T(8,128)S(1)} collective-permute-done((f32[2,2,2,16,256]{4,3,2,1,0:T(8,128)S(1)}, f32[2,2,2,16,256]{4,3,2,1,0:T(8,128)S(1)}, u32[]{:S(2)}, u32[]{:S(2)}) %collective-permute-start.15) | collective-permute-done | bytes 131104 | tf_op jit(solution)/shard_map/ppermute | solution.py:29
  88.7 5.9 %collective-permute-done.19.refs_2_ = bf16[1280,256]{1,0:T(8,128)(2,1)S(1)} collective-permute-done((bf16[1280,256]{1,0:T(8,128)(2,1)S(1)}, bf16[1280,256]{1,0:T(8,128)(2,1)S(1)}, u32[]{:S(2)}, u32[]{:S(2)}) %collective-permute-start.19) | collective-permute-done | bytes 655392 | tf_op jit(solution)/shard_map/ppermute | solution.py:25
  104.7 2.9 %collective-permute-start.24 = (f32[2,2,8,256]{3,2,1,0:T(8,128)S(1)}, f32[2,2,8,256]{3,2,1,0:T(8,128)S(1)}, u32[]{:S(2)}, u32[]{:S(2)}) collective-permute-start(f32[2,2,8,256]{3,2,1,0:T(8,128)S(1)} %shard_map.216.refs_0_), channel_id=1, source_target_pairs={{0,64},{32,96},{64,0},{96,32},{1,65},{33,97},{65,1},{97,33},{2,66}... | collective-permute-start | bytes 98312 | tf_op jit(solution)/shard_map/ppermute | solution.py:48
  109.0 3.4 %collective-permute-done.25.other = f32[2,2,2,8,256]{4,3,2,1,0:T(8,128)S(1)} collective-permute-done((f32[2,2,2,8,256]{4,3,2,1,0:T(8,128)S(1)}, f32[2,2,2,8,256]{4,3,2,1,0:T(8,128)S(1)}, u32[]{:S(2)}, u32[]{:S(2)}) %collective-permute-start.25) | collective-permute-done | bytes 65568 | tf_op jit(solution)/shard_map/ppermute | solution.py:29
  118.9 2.6 %collective-permute-done.21.refs_4_ = bf16[1280,256]{1,0:T(8,128)(2,1)S(1)} collective-permute-done((bf16[1280,256]{1,0:T(8,128)(2,1)S(1)}, bf16[1280,256]{1,0:T(8,128)(2,1)S(1)}, u32[]{:S(2)}, u32[]{:S(2)}) %collective-permute-start.21) | collective-permute-done | bytes 655392 | tf_op jit(solution)/shard_map/ppermute | solution.py:25
  122.1 3.5 %collective-permute-start.26 = (bf16[512,256]{1,0:T(8,128)(2,1)S(1)}, bf16[512,256]{1,0:T(8,128)(2,1)S(1)}, u32[]{:S(2)}, u32[]{:S(2)}) collective-permute-start(bf16[512,256]{1,0:T(8,128)(2,1)S(1)} %get-tuple-element.80), channel_id=1, source_target_pairs={{0,2},{1,3},{2,0},{3,1},{4,6},{5,7},{6,4},{7,5},{8,10},{9,11},{10,... | collective-permute-start | bytes 786440 | tf_op jit(solution)/shard_map/ppermute | solution.py:48
  125.6 8.7 %collective-permute-done.26.far = bf16[512,256]{1,0:T(8,128)(2,1)S(1)} collective-permute-done((bf16[512,256]{1,0:T(8,128)(2,1)S(1)}, bf16[512,256]{1,0:T(8,128)(2,1)S(1)}, u32[]{:S(2)}, u32[]{:S(2)}) %collective-permute-start.26) | collective-permute-done | bytes 262176 | tf_op jit(solution)/shard_map/ppermute | solution.py:48
  134.4 8.7 %collective-permute-done.27 = bf16[256,256]{1,0:T(8,128)(2,1)S(1)} collective-permute-done((bf16[256,256]{1,0:T(8,128)(2,1)S(1)}, bf16[256,256]{1,0:T(8,128)(2,1)S(1)}, u32[]{:S(2)}, u32[]{:S(2)}) %collective-permute-start.27) | collective-permute-done | bytes 131104 | tf_op jit(solution)/shard_map/ppermute | solution.py:48
  143.2 6.8 %collective-permute-done.30.refs_3_ = bf16[1296,256]{1,0:T(8,128)(2,1)S(1)} collective-permute-done((bf16[1296,256]{1,0:T(8,128)(2,1)S(1)}, bf16[1296,256]{1,0:T(8,128)(2,1)S(1)}, u32[]{:S(2)}, u32[]{:S(2)}) %collective-permute-start.30) | collective-permute-done | bytes 663584 | tf_op jit(solution)/shard_map/ppermute | solution.py:25
  150.6 3.5 %collective-permute-start.32 = (bf16[288,256]{1,0:T(8,128)(2,1)S(1)}, bf16[288,256]{1,0:T(8,128)(2,1)S(1)}, u32[]{:S(2)}, u32[]{:S(2)}) collective-permute-start(bf16[288,256]{1,0:T(8,128)(2,1)S(1)} %get-tuple-element.91), channel_id=1, source_target_pairs={{0,2},{1,3},{2,0},{3,1},{4,6},{5,7},{6,4},{7,5},{8,10},{9,11},{10,... | collective-permute-start | bytes 442376 | tf_op jit(solution)/shard_map/ppermute | solution.py:48
  158.6 9.3 %collective-permute-done.33.r3 = bf16[288,256]{1,0:T(8,128)(2,1)S(1)} collective-permute-done((bf16[288,256]{1,0:T(8,128)(2,1)S(1)}, bf16[288,256]{1,0:T(8,128)(2,1)S(1)}, u32[]{:S(2)}, u32[]{:S(2)}) %collective-permute-start.33) | collective-permute-done | bytes 147488 | tf_op jit(solution)/shard_map/ppermute | solution.py:48
  168.9 14.0 %all_to_all.5.rep = f32[16,8,256]{2,1,0:T(8,128)S(1)} all-to-all(f32[16,8,256]{2,1,0:T(8,128)S(1)} %broadcast_in_dim.30), channel_id=1, replica_groups=mesh['zl'=2,'y'=4,'core'=2,'x'=4,'zh'=4] {'zl','y','core'}, dimensions={0} | all-to-all | bytes 262144 | tf_op jit(solution)/shard_map/all_to_all | solution.py:53
  (115 shorter events, 60.5 us)
Async XLA Ops:
  3.4 24.5 %collective-permute-start.2 = (bf16[400,256]{1,0:T(8,128)(2,1)S(1)}, bf16[400,256]{1,0:T(8,128)(2,1)S(1)}, u32[]{:S(2)}, u32[]{:S(2)}) collective-permute-start(bf16[400,256]{1,0:T(8,128)(2,1)S(1)} %maximum_maximum_fusion.z0), channel_id=1, source_target_pairs={{0,3},{1,2},{2,1},{3,0},{4,7},{5,6},{6,5},{7,4},{8,11},{9,10},{10,... | collective-permute-start | bytes 614408 | tf_op jit(solution)/shard_map/ppermute | solution.py:48
  10.3 17.5 %collective-permute-start.1 = (bf16[400,256]{1,0:T(8,128)(2,1)S(1)}, bf16[400,256]{1,0:T(8,128)(2,1)S(1)}, u32[]{:S(2)}, u32[]{:S(2)}) collective-permute-start(bf16[400,256]{1,0:T(8,128)(2,1)S(1)} %maximum_maximum_fusion.z0), channel_id=1, source_target_pairs={{0,2},{1,3},{2,0},{3,1},{4,6},{5,7},{6,4},{7,5},{8,10},{9,11},{10,... | collective-permute-start | bytes 614408 | tf_op jit(solution)/shard_map/ppermute | solution.py:48
  11.3 20.4 %collective-permute-start = (bf16[400,256]{1,0:T(8,128)(2,1)S(1)}, bf16[400,256]{1,0:T(8,128)(2,1)S(1)}, u32[]{:S(2)}, u32[]{:S(2)}) collective-permute-start(bf16[400,256]{1,0:T(8,128)(2,1)S(1)} %maximum_maximum_fusion.z0), channel_id=1, source_target_pairs={{0,1},{1,0},{2,3},{3,2},{4,5},{5,4},{6,7},{7,6},{8,9},{9,8},{10,11... | collective-permute-start | bytes 614408 | tf_op jit(solution)/shard_map/ppermute | solution.py:48
  33.8 16.5 %collective-permute-start.5 = (bf16[1296,256]{1,0:T(8,128)(2,1)S(1)}, bf16[1296,256]{1,0:T(8,128)(2,1)S(1)}, u32[]{:S(2)}, u32[]{:S(2)}) collective-permute-start(bf16[1296,256]{1,0:T(8,128)(2,1)S(1)} %get-tuple-element.52.refs_0_), channel_id=1, source_target_pairs={{0,12},{4,0},{8,4},{12,8},{1,13},{5,1},{9,5},{13,9},{2,14},{6,2},{... | collective-permute-start | bytes 1990664 | tf_op jit(solution)/shard_map/ppermute | solution.py:25
  36.4 17.0 %collective-permute-start.4 = (bf16[1296,256]{1,0:T(8,128)(2,1)S(1)}, bf16[1296,256]{1,0:T(8,128)(2,1)S(1)}, u32[]{:S(2)}, u32[]{:S(2)}) collective-permute-start(bf16[1296,256]{1,0:T(8,128)(2,1)S(1)} %get-tuple-element.52.refs_0_), channel_id=1, source_target_pairs={{0,4},{4,8},{8,12},{12,0},{1,5},{5,9},{9,13},{13,1},{2,6},{6,10},{... | collective-permute-start | bytes 1990664 | tf_op jit(solution)/shard_map/ppermute | solution.py:25
  36.4 19.8 %collective-permute-start.10 = (bf16[400,256]{1,0:T(8,128)(2,1)S(1)}, bf16[400,256]{1,0:T(8,128)(2,1)S(1)}, u32[]{:S(2)}, u32[]{:S(2)}) collective-permute-start(bf16[400,256]{1,0:T(8,128)(2,1)S(1)} %shard_map.204.refs_0_.refs_5_), channel_id=1, source_target_pairs={{0,3},{1,2},{2,1},{3,0},{4,7},{5,6},{6,5},{7,4},{8,11},{9,10},{10,... | collective-permute-start | bytes 614408 | tf_op jit(solution)/shard_map/ppermute | solution.py:48
  39.1 17.1 %collective-permute-start.9 = (bf16[400,256]{1,0:T(8,128)(2,1)S(1)}, bf16[400,256]{1,0:T(8,128)(2,1)S(1)}, u32[]{:S(2)}, u32[]{:S(2)}) collective-permute-start(bf16[400,256]{1,0:T(8,128)(2,1)S(1)} %shard_map.204.refs_0_.refs_5_), channel_id=1, source_target_pairs={{0,2},{1,3},{2,0},{3,1},{4,6},{5,7},{6,4},{7,5},{8,10},{9,11},{10,... | collective-permute-start | bytes 614408 | tf_op jit(solution)/shard_map/ppermute | solution.py:48
  41.0 20.4 %collective-permute-start.8 = (bf16[400,256]{1,0:T(8,128)(2,1)S(1)}, bf16[400,256]{1,0:T(8,128)(2,1)S(1)}, u32[]{:S(2)}, u32[]{:S(2)}) collective-permute-start(bf16[400,256]{1,0:T(8,128)(2,1)S(1)} %shard_map.204.refs_0_.refs_5_), channel_id=1, source_target_pairs={{0,1},{1,0},{2,3},{3,2},{4,5},{5,4},{6,7},{7,6},{8,9},{9,8},{10,11... | collective-permute-start | bytes 614408 | tf_op jit(solution)/shard_map/ppermute | solution.py:48
  53.4 9.6 %collective-permute-start.6 = (bf16[656,256]{1,0:T(8,128)(2,1)S(1)}, bf16[656,256]{1,0:T(8,128)(2,1)S(1)}, u32[]{:S(2)}, u32[]{:S(2)}) collective-permute-start(bf16[656,256]{1,0:T(8,128)(2,1)S(1)} %get-tuple-element.53.refs_3_), channel_id=1, source_target_pairs={{0,4},{4,8},{8,12},{12,0},{1,5},{5,9},{9,13},{13,1},{2,6},{6,10},{... | collective-permute-start | bytes 1007624 | tf_op jit(solution)/shard_map/ppermute | solution.py:25
  53.5 9.5 %collective-permute-start.7 = (bf16[640,256]{1,0:T(8,128)(2,1)S(1)}, bf16[640,256]{1,0:T(8,128)(2,1)S(1)}, u32[]{:S(2)}, u32[]{:S(2)}) collective-permute-start(bf16[640,256]{1,0:T(8,128)(2,1)S(1)} %get-tuple-element.54), channel_id=1, source_target_pairs={{0,12},{4,0},{8,4},{12,8},{1,13},{5,1},{9,5},{13,9},{2,14},{6,2},{... | collective-permute-start | bytes 983048 | tf_op jit(solution)/shard_map/ppermute | solution.py:25
  63.4 25.3 %collective-permute-start.20 = (bf16[1280,256]{1,0:T(8,128)(2,1)S(1)}, bf16[1280,256]{1,0:T(8,128)(2,1)S(1)}, u32[]{:S(2)}, u32[]{:S(2)}) collective-permute-start(bf16[1280,256]{1,0:T(8,128)(2,1)S(1)} %get-tuple-element.55.refs_8_.refs_0_), channel_id=1, source_target_pairs={{0,8},{4,12},{8,0},{12,4},{1,9},{5,13},{9,1},{13,5},{2,10},{6,14},... | collective-permute-start | bytes 1966088 | tf_op jit(solution)/shard_map/ppermute | solution.py:25
  65.2 29.3 %collective-permute-start.19 = (bf16[1280,256]{1,0:T(8,128)(2,1)S(1)}, bf16[1280,256]{1,0:T(8,128)(2,1)S(1)}, u32[]{:S(2)}, u32[]{:S(2)}) collective-permute-start(bf16[1280,256]{1,0:T(8,128)(2,1)S(1)} %get-tuple-element.55.refs_8_.refs_0_), channel_id=1, source_target_pairs={{0,12},{4,0},{8,4},{12,8},{1,13},{5,1},{9,5},{13,9},{2,14},{6,2},{... | collective-permute-start | bytes 1966088 | tf_op jit(solution)/shard_map/ppermute | solution.py:25
  66.3 29.4 %collective-permute-start.18 = (bf16[1280,256]{1,0:T(8,128)(2,1)S(1)}, bf16[1280,256]{1,0:T(8,128)(2,1)S(1)}, u32[]{:S(2)}, u32[]{:S(2)}) collective-permute-start(bf16[1280,256]{1,0:T(8,128)(2,1)S(1)} %get-tuple-element.55.refs_8_.refs_0_), channel_id=1, source_target_pairs={{0,4},{4,8},{8,12},{12,0},{1,5},{5,9},{9,13},{13,1},{2,6},{6,10},{... | collective-permute-start | bytes 1966088 | tf_op jit(solution)/shard_map/ppermute | solution.py:25
  85.9 31.6 %collective-permute-start.16 = (bf16[1280,256]{1,0:T(8,128)(2,1)S(1)}, bf16[1280,256]{1,0:T(8,128)(2,1)S(1)}, u32[]{:S(2)}, u32[]{:S(2)}) collective-permute-start(bf16[1280,256]{1,0:T(8,128)(2,1)S(1)} %get-tuple-element.62), channel_id=1, source_target_pairs={{0,4},{4,8},{8,12},{12,0},{1,5},{5,9},{9,13},{13,1},{2,6},{6,10},{... | collective-permute-start | bytes 1966088 | tf_op jit(solution)/shard_map/ppermute | solution.py:25
  87.5 31.5 %collective-permute-start.17 = (bf16[1280,256]{1,0:T(8,128)(2,1)S(1)}, bf16[1280,256]{1,0:T(8,128)(2,1)S(1)}, u32[]{:S(2)}, u32[]{:S(2)}) collective-permute-start(bf16[1280,256]{1,0:T(8,128)(2,1)S(1)} %get-tuple-element.63), channel_id=1, source_target_pairs={{0,12},{4,0},{8,4},{12,8},{1,13},{5,1},{9,5},{13,9},{2,14},{6,2},{... | collective-permute-start | bytes 1966088 | tf_op jit(solution)/shard_map/ppermute | solution.py:25
  97.1 24.4 %collective-permute-start.21 = (bf16[1280,256]{1,0:T(8,128)(2,1)S(1)}, bf16[1280,256]{1,0:T(8,128)(2,1)S(1)}, u32[]{:S(2)}, u32[]{:S(2)}) collective-permute-start(bf16[1280,256]{1,0:T(8,128)(2,1)S(1)} %shard_map.214), channel_id=1, source_target_pairs={{0,8},{4,12},{8,0},{12,4},{1,9},{5,13},{9,1},{13,5},{2,10},{6,14},... | collective-permute-start | bytes 1966088 | tf_op jit(solution)/shard_map/ppermute | solution.py:25
  114.8 28.4 %collective-permute-start.28 = (bf16[1296,256]{1,0:T(8,128)(2,1)S(1)}, bf16[1296,256]{1,0:T(8,128)(2,1)S(1)}, u32[]{:S(2)}, u32[]{:S(2)}) collective-permute-start(bf16[1296,256]{1,0:T(8,128)(2,1)S(1)} %get-tuple-element.84), channel_id=1, source_target_pairs={{0,4},{4,8},{8,12},{12,0},{1,5},{5,9},{9,13},{13,1},{2,6},{6,10},{... | collective-permute-start | bytes 1990664 | tf_op jit(solution)/shard_map/ppermute | solution.py:25
  115.3 27.9 %collective-permute-start.29 = (bf16[1296,256]{1,0:T(8,128)(2,1)S(1)}, bf16[1296,256]{1,0:T(8,128)(2,1)S(1)}, u32[]{:S(2)}, u32[]{:S(2)}) collective-permute-start(bf16[1296,256]{1,0:T(8,128)(2,1)S(1)} %get-tuple-element.85), channel_id=1, source_target_pairs={{0,12},{4,0},{8,4},{12,8},{1,13},{5,1},{9,5},{13,9},{2,14},{6,2},{... | collective-permute-start | bytes 1990664 | tf_op jit(solution)/shard_map/ppermute | solution.py:25
  117.5 32.4 %collective-permute-start.30 = (bf16[1296,256]{1,0:T(8,128)(2,1)S(1)}, bf16[1296,256]{1,0:T(8,128)(2,1)S(1)}, u32[]{:S(2)}, u32[]{:S(2)}) collective-permute-start(bf16[1296,256]{1,0:T(8,128)(2,1)S(1)} %get-tuple-element.86), channel_id=1, source_target_pairs={{0,8},{4,12},{8,0},{12,4},{1,9},{5,13},{9,1},{13,5},{2,10},{6,14},... | collective-permute-start | bytes 1990664 | tf_op jit(solution)/shard_map/ppermute | solution.py:25
  122.1 12.2 %collective-permute-start.26 = (bf16[512,256]{1,0:T(8,128)(2,1)S(1)}, bf16[512,256]{1,0:T(8,128)(2,1)S(1)}, u32[]{:S(2)}, u32[]{:S(2)}) collective-permute-start(bf16[512,256]{1,0:T(8,128)(2,1)S(1)} %get-tuple-element.80), channel_id=1, source_target_pairs={{0,2},{1,3},{2,0},{3,1},{4,6},{5,7},{6,4},{7,5},{8,10},{9,11},{10,... | collective-permute-start | bytes 786440 | tf_op jit(solution)/shard_map/ppermute | solution.py:48
  134.3 8.8 %collective-permute-start.27 = (bf16[256,256]{1,0:T(8,128)(2,1)S(1)}, bf16[256,256]{1,0:T(8,128)(2,1)S(1)}, u32[]{:S(2)}, u32[]{:S(2)}) collective-permute-start(bf16[256,256]{1,0:T(8,128)(2,1)S(1)} %get-tuple-element.82), channel_id=1, source_target_pairs={{0,1},{1,0},{2,3},{3,2},{4,5},{5,4},{6,7},{7,6},{8,9},{9,8},{10,11... | collective-permute-start | bytes 393224 | tf_op jit(solution)/shard_map/ppermute | solution.py:48
  150.4 6.3 %collective-permute-start.31 = (bf16[288,256]{1,0:T(8,128)(2,1)S(1)}, bf16[288,256]{1,0:T(8,128)(2,1)S(1)}, u32[]{:S(2)}, u32[]{:S(2)}) collective-permute-start(bf16[288,256]{1,0:T(8,128)(2,1)S(1)} %get-tuple-element.90), channel_id=1, source_target_pairs={{0,1},{1,0},{2,3},{3,2},{4,5},{5,4},{6,7},{7,6},{8,9},{9,8},{10,11... | collective-permute-start | bytes 442376 | tf_op jit(solution)/shard_map/ppermute | solution.py:48
  150.6 8.0 %collective-permute-start.32 = (bf16[288,256]{1,0:T(8,128)(2,1)S(1)}, bf16[288,256]{1,0:T(8,128)(2,1)S(1)}, u32[]{:S(2)}, u32[]{:S(2)}) collective-permute-start(bf16[288,256]{1,0:T(8,128)(2,1)S(1)} %get-tuple-element.91), channel_id=1, source_target_pairs={{0,2},{1,3},{2,0},{3,1},{4,6},{5,7},{6,4},{7,5},{8,10},{9,11},{10,... | collective-permute-start | bytes 442376 | tf_op jit(solution)/shard_map/ppermute | solution.py:48
  154.1 13.8 %collective-permute-start.33 = (bf16[288,256]{1,0:T(8,128)(2,1)S(1)}, bf16[288,256]{1,0:T(8,128)(2,1)S(1)}, u32[]{:S(2)}, u32[]{:S(2)}) collective-permute-start(bf16[288,256]{1,0:T(8,128)(2,1)S(1)} %get-tuple-element.92), channel_id=1, source_target_pairs={{0,3},{1,2},{2,1},{3,0},{4,7},{5,6},{6,5},{7,4},{8,11},{9,10},{10,... | collective-permute-start | bytes 442376 | tf_op jit(solution)/shard_map/ppermute | solution.py:48
  (29 other events, 458.2 us)
